TPU v7x, 32 devices: a whole 2x2x4 slice. The times are simulated.
32 devices in a mesh: rows: 8 (over z, y), rhs: 4 (over x, core).
Axes of the slice: x: 2, y: 2, z: 4, core: 2. Of those that a mesh axis runs over, the one named last changes fastest.
Arguments:
- factor_left: bfloat16 [1024, 128, 128], P(('rows', 'rhs')), may hold values from -0.5 to 0.5
- factor_right: bfloat16 [1024, 128, 128], P(('rows', 'rhs')), may hold values from -0.5 to 0.5
- state_diag: float32 [1024, 128], P(('rows', 'rhs')), may hold values from 0.02 to 0.2
- owner: int32 [1024, 1], P(('rows', 'rhs')), may hold values from 0 to 7; in each aligned block of 32 rows (0 to 31, 32 to 63, ...) at most 12 rows name the same one
- col_local: int32 [1024], P(('rows', 'rhs')), may hold values from 0 to 15
- row_shift: int32 [1024], P(('rows', 'rhs')), may hold values from 0 to 2
- row_local: int32 [1024], P(('rows', 'rhs')), may hold values from 0 to 15
- rhs_in: float32 [128, 256, 128], P('rows', 'rhs'), may hold values from -6 to 6
- low_bound: float32 [1], replicated, may hold values from 0.55 to 0.7
- high_bound: float32 [1], replicated, may hold values from 1.3 to 1.5
Outputs:
- adjoint: float32 [128, 256, 128], P('rows', 'rhs')
- residual: float32 [128, 256, 128], P('rows', 'rhs')
Inputs may be any that keep to these rules, and one draw needn't show every extreme that they name: Among the 32 blocks of one device no owner is named more than 12 times, and every draw has a device that names some owner 12 times.
All inputs are finite; a program needn't handle non-finite values.
Results may differ from a plain program's by a relative error of at most 0.0082.
Values may be sent and summed in bfloat16 or wider, within the bound.
A program may use at most 128 MiB of HBM per device.

v0:
```python
import functools

import jax
import jax.numpy as jnp
from jax import lax
from jax.experimental import pallas as pl
from jax.experimental.pallas import tpu as pltpu
from jax.sharding import PartitionSpec as P

ITERS = 4
GROUP = 16
BUFFERS = 4
VMEM_LIMIT = 54 * 1024 * 1024
MESH = pl.DeviceIdType.MESH


def bits_of(local_rows):
    return (2 * local_rows).bit_length(), local_rows.bit_length()


def form_kernel(room, left_ref, right_ref, diag_ref, dest_ref, col_ref, shift_ref, row_ref, rows_ref, send_ref, notes, filled):
    slots, width, _ = left_ref.shape
    peers = send_ref.shape[0]
    notes[...] = jnp.zeros_like(notes)
    for owner in range(peers):
        filled[owner] = 0
    line = lax.broadcasted_iota(jnp.int32, notes.shape[1:], 0)
    lane = lax.broadcasted_iota(jnp.int32, notes.shape[1:], 1)
    for k in range(slots):
        scaled = (diag_ref[:, k : k + 1] * right_ref[k].astype(jnp.float32)).astype(jnp.bfloat16)
        block = jnp.dot(left_ref[k], scaled, preferred_element_type=jnp.float32)
        owner = dest_ref[k]
        place = filled[owner]
        filled[owner] = place + 1
        send_ref[owner, pl.ds(pl.multiple_of(place * width, width), width)] = block.astype(jnp.bfloat16)
        shift = shift_ref[k]
        index = row_ref[k] + jnp.where(shift == 2, rows_ref[0], 0)
        near = jnp.where(shift == 1, 1, 0)
        note = jnp.where(line == 0, 1, jnp.where(line == 1, col_ref[k], jnp.where(line == 2, index, near)))
        notes[owner] = jnp.where((lane == place) & (line < 4), note, notes[owner])
    for owner in range(peers):
        send_ref[owner, room * width : room * width + 16] = notes[owner].astype(jnp.float32).astype(jnp.bfloat16)


def form(left, right, diag, dest, col, shift, row, local_rows, peers, room):
    slots, width, _ = left.shape
    smem = pl.BlockSpec(memory_space=pltpu.SMEM)
    vmem = pl.BlockSpec(memory_space=pltpu.VMEM)
    return pl.pallas_call(
        functools.partial(form_kernel, room),
        out_shape=jax.ShapeDtypeStruct((peers, room * width + 16, width), jnp.bfloat16),
        in_specs=[vmem, vmem, vmem, smem, smem, smem, smem, smem],
        out_specs=vmem,
        scratch_shapes=[
            pltpu.VMEM((peers, 16, width), jnp.int32),
            pltpu.SMEM((peers,), jnp.int32),
        ],
        compiler_params=pltpu.CompilerParams(vmem_limit_bytes=VMEM_LIMIT),
        name="form",
    )(left, right, diag.T, dest, col, shift, row, jnp.full((1,), local_rows, jnp.int32))


def route_kernel(peers, sides, pieces, send_ref, got_ref, own_sem, send_sems, recv_sems):
    me, side = lax.axis_index("rows"), lax.axis_index("rhs")
    across, beside = side ^ 2, side ^ 1
    paired = peers & (peers - 1) == 0

    def target(d):
        return me ^ d if paired else lax.rem(me + d, peers)

    def source(d):
        return me ^ d if paired else lax.rem(me - d + peers, peers)

    barrier = pltpu.get_barrier_semaphore()
    for d in range(1, peers):
        pl.semaphore_signal(barrier, inc=1, device_id=(source(d), side), device_id_type=MESH)
    for other in (across, beside):
        pl.semaphore_signal(barrier, inc=1, device_id=(me, other), device_id_type=MESH)
    pl.semaphore_wait(barrier, peers + 1)

    def remote(kind, d, piece, src, slot, device):
        begin, end = pieces[piece]
        return pltpu.make_async_remote_copy(
            src_ref=src.at[begin:end],
            dst_ref=got_ref.at[slot, begin:end],
            send_sem=send_sems.at[kind, d, piece],
            recv_sem=recv_sems.at[kind, d, piece],
            device_id=device,
            device_id_type=MESH,
        )

    def to_owner(d, p):
        return remote(0, d, p, send_ref.at[target(d)], me * sides + side, (target(d), side))

    def held(d):
        return send_ref.at[me] if d == 0 else got_ref.at[source(d) * sides + side]

    def to_across(d, p):
        return remote(1, d, p, held(d), source(d) * sides + side, (me, across))

    def to_beside(d, p):
        return remote(2, d, p, held(d), source(d) * sides + side, (me, beside))

    def on_beside(d, p):
        slot = source(d) * sides + across
        return remote(3, d, p, got_ref.at[slot], slot, (me, beside))

    count = len(pieces)
    near = [(d, p) for d in range(1, peers // 2) for p in range(count)]
    far = [(d, p) for d in range(peers // 2, peers) for p in range(count)]
    follow = {}
    for queue in (near, far):
        follow.update(zip(queue, queue[2:]))
    for item in far[:2] + near[:2]:
        to_owner(*item).start()
    own = pltpu.make_async_copy(send_ref.at[me], got_ref.at[me * sides + side], own_sem)
    own.start()
    order = [(0, p) for p in range(count)]
    while near or far:
        order += near[:2] + far[:1]
        near, far = near[2:], far[1:]
    for step in range(len(order) + 2):
        if step < len(order):
            item = order[step]
            if item[0] > 0:
                to_owner(*item).wait_recv()
            to_across(*item).start()
            to_beside(*item).start()
            if item in follow:
                to_owner(*item).wait_send()
                to_owner(*follow[item]).start()
        if step >= 2:
            to_across(*order[step - 2]).wait_recv()
            on_beside(*order[step - 2]).start()
    own.wait()
    for item in order:
        if item[0] > 0 and item not in follow:
            to_owner(*item).wait_send()
        to_across(*item).wait_send()
        to_beside(*item).wait()
        on_beside(*item).wait()


def route(send, peers, sides, room):
    rows, width = send.shape[1:]
    if peers > 16 or room < 2:
        pieces = ((0, rows),)
    else:
        pieces = ((0, room // 2 * width), (room // 2 * width, rows))
    return pl.pallas_call(
        functools.partial(route_kernel, peers, sides, pieces),
        out_shape=jax.ShapeDtypeStruct((peers * sides, rows, width), send.dtype),
        in_specs=[pl.BlockSpec(memory_space=pltpu.HBM)],
        out_specs=pl.BlockSpec(memory_space=pltpu.HBM),
        scratch_shapes=[
            pltpu.SemaphoreType.DMA,
            pltpu.SemaphoreType.DMA((4, peers, len(pieces))),
            pltpu.SemaphoreType.DMA((4, peers, len(pieces))),
        ],
        compiler_params=pltpu.CompilerParams(collective_id=0, has_side_effects=True),
        name="route",
    )(send)


def block_lists(notes, room, local_rows):
    index_bits, col_bits = bits_of(local_rows)
    filled, col, index, near = [notes[:, i, :room].reshape(-1) for i in range(4)]
    count = filled.shape[0]
    length = -(-(count + 2 * local_rows) // GROUP) * GROUP
    key = jnp.where(filled == 1, (1 - near) * local_rows + col, -1)
    items = jnp.arange(count)
    keys = jnp.arange(2 * local_rows)
    rank = jnp.sum(
        ((key[:, None] == key[None, :]) & (items[None, :] < items[:, None])).astype(jnp.int32), axis=1
    )
    is_key = key[:, None] == keys[None, :]
    even = (jnp.sum(is_key.astype(jnp.int32), axis=0) + 1) // 2 * 2
    near_key = keys < local_rows
    before = (keys[:, None] > keys[None, :]) & (near_key[:, None] == near_key[None, :])
    first = jnp.sum(jnp.where(before, even[None, :], 0), axis=1)
    pos = rank + jnp.sum(jnp.where(is_key, first[None, :], 0), axis=1)
    value = ((items << col_bits) | col) << index_bits | index
    some = jnp.max(jnp.where(filled == 1, items, 0))
    empty = ((some << col_bits) | local_rows) << index_bits | (2 * local_rows)

    def listed(chosen):
        pick = jnp.arange(length)[:, None] == jnp.where(chosen, pos, -1)[None, :]
        return empty + jnp.sum(jnp.where(pick, value[None, :] - empty, 0), axis=1)

    near_half = listed((key >= 0) & (key < local_rows))
    far_half = listed(key >= local_rows)
    near_count = jnp.sum(jnp.where(near_key, even, 0)).reshape(1)
    far_count = jnp.sum(jnp.where(near_key, 0, even)).reshape(1)
    return near_half, near_count, far_half, far_count


def add_blocks(first_sweep, room, list_ref, count_ref, blocks_ref, packed_ref, ext, acc, buf, sems, local_rows):
    index_bits, col_bits = bits_of(local_rows)
    width = buf.shape[-1]
    chunks = lax.div(count_ref[0] + (GROUP - 1), jnp.int32(GROUP))

    def copies(chunk):
        slot = lax.rem(chunk, BUFFERS)
        if not first_sweep:
            return [
                pltpu.make_async_copy(
                    packed_ref.at[pl.ds(chunk * GROUP * width, GROUP * width)], buf.at[slot], sems.at[slot, 0]
                )
            ]
        out = []
        for g in range(GROUP):
            item = list_ref[chunk * GROUP + g] >> (index_bits + col_bits)
            part = lax.div(item, jnp.int32(room))
            place = item - part * room
            out.append(
                pltpu.make_async_copy(
                    blocks_ref.at[part, pl.ds(pl.multiple_of(place * width, width), width)],
                    buf.at[slot, g * width : (g + 1) * width],
                    sems.at[slot, g],
                )
            )
        return out

    def write(chunk):
        slot = lax.rem(chunk, BUFFERS)
        return pltpu.make_async_copy(
            buf.at[slot], packed_ref.at[pl.ds(chunk * GROUP * width, GROUP * width)], sems.at[slot, GROUP]
        )

    def start(chunk):
        @pl.when(chunk < chunks)
        def _():
            for copy in copies(chunk):
                copy.start()

    for ahead in range(BUFFERS - 1):
        start(jnp.int32(ahead))

    def body(chunk, carry):
        if first_sweep:

            @pl.when(chunk > 0)
            def _():
                write(chunk - 1).wait()

        start(chunk + (BUFFERS - 1))
        for copy in copies(chunk):
            copy.wait()
        if first_sweep:
            write(chunk).start()
        slot = lax.rem(chunk, BUFFERS)
        mask = (1 << index_bits) - 1
        for g in range(0, GROUP, 2):
            item = list_ref[chunk * GROUP + g]
            other = list_ref[chunk * GROUP + g + 1]
            col = (item >> index_bits) & ((1 << col_bits) - 1)
            rows = jnp.concatenate([ext[item & mask], ext[other & mask]], axis=1)
            pair = buf[slot, g * width : (g + 2) * width]
            acc[col] += jnp.dot(rows, pair, preferred_element_type=jnp.float32)
        return carry

    lax.fori_loop(0, chunks, body, 0)
    if first_sweep:

        @pl.when(chunks > 0)
        def _():
            write(chunks - 1).wait()


def near_kernel(first_sweep, room, list_ref, count_ref, blocks_ref, own_ref, dir_ref, res_ref, *rest):
    if first_sweep:
        out_ref, packed_ref, ext, acc, buf, sems = rest
    else:
        out_ref, ext, acc, buf, sems = rest
        packed_ref = blocks_ref
    rows = dir_ref.shape[0]
    acc[0:rows] = res_ref[...] - dir_ref[...]
    ext[0:rows] = own_ref[...]
    ext[2 * rows] = jnp.zeros_like(ext[0])
    add_blocks(first_sweep, room, list_ref, count_ref, blocks_ref, packed_ref, ext, acc, buf, sems, rows)
    out_ref[...] = acc[0:rows]


def far_kernel(first_sweep, last, room, list_ref, count_ref, coef_ref, blocks_ref, low_ref, high_ref, part_ref, *rest):
    *refs, ext, acc, buf, sems, ext_sems = rest
    packed_ref = refs.pop() if first_sweep else blocks_ref
    if last:
        (res_out,) = refs
    else:
        dir_ref, adj_ref, res_out, dir_out, adj_out, round_out = refs
    rows = part_ref.shape[0]
    low = pltpu.make_async_copy(low_ref, ext.at[0:rows], ext_sems.at[0])
    high = pltpu.make_async_copy(high_ref, ext.at[rows : 2 * rows], ext_sems.at[1])
    low.start()
    high.start()
    acc[0:rows] = part_ref[...]
    ext[2 * rows] = jnp.zeros_like(part_ref[0]).astype(jnp.bfloat16)
    low.wait()
    high.wait()
    add_blocks(first_sweep, room, list_ref, count_ref, blocks_ref, packed_ref, ext, acc, buf, sems, rows)
    res = acc[0:rows]
    res_out[...] = res
    if not last:
        direction = coef_ref[0] * dir_ref[...] + coef_ref[1] * res
        dir_out[...] = direction
        adj_out[...] = adj_ref[...] + direction
        round_out[...] = direction.astype(jnp.bfloat16)


def local(
    factor_left,
    factor_right,
    state_diag,
    owner,
    col_local,
    row_shift,
    row_local,
    rhs_in,
    low_bound,
    high_bound,
):
    peers = lax.axis_size("rows")
    sides = lax.axis_size("rhs")
    slots = owner.shape[0]
    width = factor_left.shape[1]
    local_rows, columns, _ = rhs_in.shape
    room = min(slots, max(2, 3 * slots // peers))
    dest = owner[:, 0]

    send = form(
        factor_left, factor_right, state_diag, dest, col_local, row_shift, row_local, local_rows, peers, room
    )
    got = route(send, peers, sides, room)
    notes = got[:, room * width :, :].astype(jnp.int32)
    near_list, near_count, far_list, far_count = block_lists(notes, room, local_rows)
    packed_shape = jax.ShapeDtypeStruct((near_list.shape[0] * width, width), jnp.bfloat16)

    low = low_bound[0]
    high = high_bound[0]
    theta = (high + low) / 2.0
    delta = (high - low) / 2.0
    sigma = theta / delta
    rho = 1.0 / sigma
    residual = rhs_in
    direction = residual / theta
    adjoint = direction
    rounded = direction.astype(jnp.bfloat16)

    forward = [(i, (i + 1) % peers) for i in range(peers)]
    backward = [(i, (i - 1) % peers) for i in range(peers)]
    smem = pl.BlockSpec(memory_space=pltpu.SMEM)
    vmem = pl.BlockSpec(memory_space=pltpu.VMEM)
    hbm = pl.BlockSpec(memory_space=pltpu.HBM)
    anywhere = pl.BlockSpec(memory_space=pl.ANY)
    field = jax.ShapeDtypeStruct(rhs_in.shape, jnp.float32)
    work = [
        pltpu.VMEM((2 * local_rows + 1, columns, width), jnp.bfloat16),
        pltpu.VMEM((local_rows + 1, columns, width), jnp.float32),
        pltpu.VMEM((BUFFERS, GROUP * width, width), jnp.bfloat16),
        pltpu.SemaphoreType.DMA((BUFFERS, GROUP + 1)),
    ]
    params = pltpu.CompilerParams(vmem_limit_bytes=VMEM_LIMIT)

    def cost(amount):
        return pl.CostEstimate(
            flops=2 * amount * columns * width * width,
            bytes_accessed=amount * width * width * 2 + 4 * rhs_in.size * 4,
            transcendentals=0,
        )

    near_blocks, far_blocks = got, got
    for sweep in range(ITERS):
        first_sweep, last = sweep == 0, sweep + 1 == ITERS
        low_rows = lax.ppermute(rounded, "rows", forward)
        high_rows = lax.ppermute(rounded, "rows", backward)
        result = pl.pallas_call(
            functools.partial(near_kernel, first_sweep, room),
            out_shape=[field] + [packed_shape] * first_sweep,
            in_specs=[smem, smem, hbm, vmem, vmem, vmem],
            out_specs=[vmem] + [hbm] * first_sweep,
            scratch_shapes=work,
            compiler_params=params,
            cost_estimate=cost(near_list.shape[0] // 4),
            name="near_first" if first_sweep else "near",
        )(near_list, near_count, near_blocks, rounded, direction, residual)
        part = result[0]
        if first_sweep:
            near_blocks = result[1]
        if last:
            coef = jnp.zeros((2,), jnp.float32)
        else:
            rho_next = 1.0 / (2.0 * sigma - rho)
            coef = jnp.stack([rho_next * rho, 2.0 * rho_next / delta])
            rho = rho_next
        fields = [] if last else [direction, adjoint]
        outs = [field] if last else [field] * 3 + [jax.ShapeDtypeStruct(rhs_in.shape, jnp.bfloat16)]
        result = pl.pallas_call(
            functools.partial(far_kernel, first_sweep, last, room),
            out_shape=outs + [packed_shape] * first_sweep,
            in_specs=[smem, smem, smem, hbm, anywhere, anywhere, vmem] + [vmem] * len(fields),
            out_specs=[vmem] * len(outs) + [hbm] * first_sweep,
            scratch_shapes=work + [pltpu.SemaphoreType.DMA((2,))],
            compiler_params=params,
            cost_estimate=cost(near_list.shape[0] // 2),
            name="far_last" if last else "far_first" if first_sweep else "far",
        )(far_list, far_count, coef, far_blocks, low_rows, high_rows, part, *fields)
        residual = result[0]
        if first_sweep:
            far_blocks = result[-1]
        if not last:
            direction, adjoint, rounded = result[1:4]
    return (adjoint, residual)


def solution(mesh):
    placed = (
        P(("rows", "rhs"), None, None),
        P(("rows", "rhs"), None, None),
        P(("rows", "rhs"), None),
        P(("rows", "rhs"), None),
        P(("rows", "rhs")),
        P(("rows", "rhs")),
        P(("rows", "rhs")),
        P("rows", "rhs", None),
        P(),
        P(),
    )
    return jax.shard_map(
        local,
        mesh=mesh,
        in_specs=placed,
        out_specs=(P("rows", "rhs", None), P("rows", "rhs", None)),
        check_vma=False,
    )
```

profile of v0, /device:TPU:12, one launch (start us, length us, event | category | flops | bytes accessed | tf_op | source)
XLA Modules:
  0.0 212.4 jit_solution(3387511844291005538)
XLA Ops:
  1.9 1.9 fusion.6
  4.4 2.4 %collective-permute-start = (bf16[16,64,128]{2,1,0:T(8,128)(2,1)S(1)}, bf16[16,64,128]{2,1,0:T(8,128)(2,1)S(1)}, u32[]{:S(2)}, u32[]{:S(2)}) collective-permute-start(bf16[16,64,128]{2,1,0:T(8,128)(2,1)S(1)} %get-tuple-element.40.own_ref), channel_id=1, source_target_pairs={{0,4},{4,8},{8,12},{12,16},{16,20},{20,24},{24,28},{28,0},{1,5},{5... | collective-permute-start | bytes 786440 | tf_op jit(solution)/shard_map/ppermute | solution.py:374
  6.9 1.4 copy.14
  8.4 4.1 %form.1.send_ref = bf16[8,1552,128]{2,1,0:T(8,128)(2,1)} custom-call(bf16[32,128,128]{2,1,0:T(8,128)(2,1)} %left_ref.1, bf16[32,128,128]{2,1,0:T(8,128)(2,1)} %right_ref.1, f32[128,32]{1,0:T(8,128)} %bitcast.12, s32[32]{0:T(128)} %bitcast.13, s32[32]{0:T(128)} %col_ref.1, s32[32]{0:T(128)} %shift_ref.1, s32[32]{0:T(128)} %row_ref.1, s32[1]{0:T(128)} %constant.15.clone.1.rows_ref), custom_call_target="tpu_custom_call" | custom-call | tf_op jit(solution)/shard_map/form/pallas_call | solution.py:49
  12.5 85.6 %route.1.blocks_ref = bf16[32,1552,128]{2,1,0:T(8,128)(2,1)} custom-call(bf16[8,1552,128]{2,1,0:T(8,128)(2,1)} %form.1.send_ref), custom_call_target="tpu_custom_call" | custom-call | tf_op jit(solution)/shard_map/route/pallas_call | solution.py:150
  98.1 0.9 slice_convert_fusion
  99.1 0.8 fusion.2
  101.4 0.7 select_reduce_fusion.4
  103.2 11.6 %near_first.1 = (f32[16,64,128]{2,1,0:T(8,128)}, bf16[53248,128]{1,0:T(8,128)(2,1)}) custom-call(s32[416]{0:T(512)} %get-tuple-element.47.list_ref, s32[1]{0:T(128)} %bitcast.9.count_ref, bf16[32,1552,128]{2,1,0:T(8,128)(2,1)} %route.1.blocks_ref, bf16[16,64,128]{2,1,0:T(8,128)(2,1)} %copy-done, f32[16,64,128]{2,1,0:T(8,128)} %get-tuple-element.41.dir_ref.rest_0_.rest_1_, ...), custom_call_target="tpu_custom_call" | custom-call | flops 218103808 | bytes 5505024 | tf_op jit(solution)/shard_map/near_first/pallas_call | solution.py:376
  116.3 20.2 %far_first.1 = (f32[16,64,128]{2,1,0:T(8,128)}, f32[16,64,128]{2,1,0:T(8,128)}, f32[16,64,128]{2,1,0:T(8,128)}, bf16[16,64,128]{2,1,0:T(8,128)(2,1)}, bf16[53248,128]{1,0:T(8,128)(2,1)}) custom-call(s32[416]{0:T(512)} %get-tuple-element.48.list_ref, s32[1]{0:T(128)} %bitcast.2.count_ref, f32[2]{0:T(128)} %pad_maximum_fusion.1.coef_ref, ...), custom_call_target="tpu_custom_call" | custom-call | flops 436207616 | bytes 8912896 | tf_op jit(solution)/shard_map/far_first/pallas_call | solution.py:397
  136.6 2.9 %collective-permute-start.2 = (bf16[16,64,128]{2,1,0:T(8,128)(2,1)}, bf16[16,64,128]{2,1,0:T(8,128)(2,1)S(1)}, u32[]{:S(2)}, u32[]{:S(2)}) collective-permute-start(bf16[16,64,128]{2,1,0:T(8,128)(2,1)} %get-tuple-element.19.own_ref), channel_id=1, source_target_pairs={{0,4},{4,8},{8,12},{12,16},{16,20},{20,24},{24,28},{28,0},{1,5},{5... | collective-permute-start | bytes 786440 | tf_op jit(solution)/shard_map/ppermute | solution.py:374
  140.2 6.8 %near.3.part_ref = f32[16,64,128]{2,1,0:T(8,128)} custom-call(s32[416]{0:T(512)} %get-tuple-element.47.list_ref, s32[1]{0:T(128)} %bitcast.9.count_ref, bf16[53248,128]{1,0:T(8,128)(2,1)} %get-tuple-element.20.blocks_ref, bf16[16,64,128]{2,1,0:T(8,128)(2,1)} %get-tuple-element.19.own_ref, f32[16,64,128]{2,1,0:T(8,128)} %get-tuple-element.21.dir_ref.rest_0_, ...), custom_call_target="tpu_custom_call" | custom-call | flops 218103808 | bytes 5505024 | tf_op jit(solution)/shard_map/near/pallas_call | solution.py:376
  147.0 4.1 %collective-permute-done.2.low_ref = bf16[16,64,128]{2,1,0:T(8,128)(2,1)S(1)} collective-permute-done((bf16[16,64,128]{2,1,0:T(8,128)(2,1)}, bf16[16,64,128]{2,1,0:T(8,128)(2,1)S(1)}, u32[]{:S(2)}, u32[]{:S(2)}) %collective-permute-start.2) | collective-permute-done | bytes 262176 | tf_op jit(solution)/shard_map/ppermute | solution.py:374
  151.1 0.7 copy-done.6
  151.8 11.0 %far.2 = (f32[16,64,128]{2,1,0:T(8,128)}, f32[16,64,128]{2,1,0:T(8,128)}, f32[16,64,128]{2,1,0:T(8,128)}, bf16[16,64,128]{2,1,0:T(8,128)(2,1)}) custom-call(s32[416]{0:T(512)} %get-tuple-element.48.list_ref, s32[1]{0:T(128)} %bitcast.2.count_ref, f32[2]{0:T(128)} %pad_maximum_fusion.2.coef_ref, bf16[53248,128]{1,0:T(8,128)(2,1)} %get-tuple-element.18.blocks_ref, ...), custom_call_target="tpu_custom_call" | custom-call | flops 436207616 | bytes 8912896 | tf_op jit(solution)/shard_map/far/pallas_call | solution.py:397
  162.8 2.9 %collective-permute-start.4 = (bf16[16,64,128]{2,1,0:T(8,128)(2,1)}, bf16[16,64,128]{2,1,0:T(8,128)(2,1)S(1)}, u32[]{:S(2)}, u32[]{:S(2)}) collective-permute-start(bf16[16,64,128]{2,1,0:T(8,128)(2,1)} %get-tuple-element.24.own_ref), channel_id=1, source_target_pairs={{0,4},{4,8},{8,12},{12,16},{16,20},{20,24},{24,28},{28,0},{1,5},{5... | collective-permute-start | bytes 786440 | tf_op jit(solution)/shard_map/ppermute | solution.py:374
  166.4 6.8 %near.4.part_ref = f32[16,64,128]{2,1,0:T(8,128)} custom-call(s32[416]{0:T(512)} %get-tuple-element.47.list_ref, s32[1]{0:T(128)} %bitcast.9.count_ref, bf16[53248,128]{1,0:T(8,128)(2,1)} %get-tuple-element.20.blocks_ref, bf16[16,64,128]{2,1,0:T(8,128)(2,1)} %get-tuple-element.24.own_ref, f32[16,64,128]{2,1,0:T(8,128)} %get-tuple-element.25.dir_ref.rest_0_, ...), custom_call_target="tpu_custom_call" | custom-call | flops 218103808 | bytes 5505024 | tf_op jit(solution)/shard_map/near/pallas_call | solution.py:376
  173.2 3.3 %collective-permute-done.4.low_ref = bf16[16,64,128]{2,1,0:T(8,128)(2,1)S(1)} collective-permute-done((bf16[16,64,128]{2,1,0:T(8,128)(2,1)}, bf16[16,64,128]{2,1,0:T(8,128)(2,1)S(1)}, u32[]{:S(2)}, u32[]{:S(2)}) %collective-permute-start.4) | collective-permute-done | bytes 262176 | tf_op jit(solution)/shard_map/ppermute | solution.py:374
  176.5 0.7 copy-done.4
  177.2 11.0 %far.3 = (f32[16,64,128]{2,1,0:T(8,128)}, f32[16,64,128]{2,1,0:T(8,128)}, f32[16,64,128]{2,1,0:T(8,128)}, bf16[16,64,128]{2,1,0:T(8,128)(2,1)}) custom-call(s32[416]{0:T(512)} %get-tuple-element.48.list_ref, s32[1]{0:T(128)} %bitcast.2.count_ref, f32[2]{0:T(128)} %pad_maximum_fusion.coef_ref, bf16[53248,128]{1,0:T(8,128)(2,1)} %get-tuple-element.18.blocks_ref, ...), custom_call_target="tpu_custom_call" | custom-call | flops 436207616 | bytes 8912896 | tf_op jit(solution)/shard_map/far/pallas_call | solution.py:397
  188.3 2.9 %collective-permute-start.6 = (bf16[16,64,128]{2,1,0:T(8,128)(2,1)}, bf16[16,64,128]{2,1,0:T(8,128)(2,1)S(1)}, u32[]{:S(2)}, u32[]{:S(2)}) collective-permute-start(bf16[16,64,128]{2,1,0:T(8,128)(2,1)} %get-tuple-element.29.own_ref), channel_id=1, source_target_pairs={{0,4},{4,8},{8,12},{12,16},{16,20},{20,24},{24,28},{28,0},{1,5},{5... | collective-permute-start | bytes 786440 | tf_op jit(solution)/shard_map/ppermute | solution.py:374
  191.2 6.8 %near.5.part_ref = f32[16,64,128]{2,1,0:T(8,128)} custom-call(s32[416]{0:T(512)} %get-tuple-element.47.list_ref, s32[1]{0:T(128)} %bitcast.9.count_ref, bf16[53248,128]{1,0:T(8,128)(2,1)} %get-tuple-element.20.blocks_ref, bf16[16,64,128]{2,1,0:T(8,128)(2,1)} %get-tuple-element.29.own_ref, f32[16,64,128]{2,1,0:T(8,128)} %get-tuple-element.30.dir_ref, ...), custom_call_target="tpu_custom_call" | custom-call | flops 218103808 | bytes 5505024 | tf_op jit(solution)/shard_map/near/pallas_call | solution.py:376
  198.0 3.5 %collective-permute-done.6.low_ref = bf16[16,64,128]{2,1,0:T(8,128)(2,1)S(1)} collective-permute-done((bf16[16,64,128]{2,1,0:T(8,128)(2,1)}, bf16[16,64,128]{2,1,0:T(8,128)(2,1)S(1)}, u32[]{:S(2)}, u32[]{:S(2)}) %collective-permute-start.6) | collective-permute-done | bytes 262176 | tf_op jit(solution)/shard_map/ppermute | solution.py:374
  202.2 10.2 %far_last.1 = f32[16,64,128]{2,1,0:T(8,128)} custom-call(s32[416]{0:T(512)} %get-tuple-element.48.list_ref, s32[1]{0:T(128)} %bitcast.2.count_ref, f32[2]{0:T(128)} %broadcast_3_coef_ref.2.coef_ref, bf16[53248,128]{1,0:T(8,128)(2,1)} %get-tuple-element.18.blocks_ref, bf16[16,64,128]{2,1,0:T(8,128)(2,1)} %copy-done.8, bf16[16,64,128]{2,1,0:T(8,128)(2,1)} %copy-done.7, ...), custom_call_target="tpu_custom_call" | custom-call | flops 436207616 | bytes 8912896 | tf_op jit(solution)/shard_map/far_last/pallas_call | solution.py:397
  (43 shorter events, 5.9 us)
Async XLA Ops:
  3.9 99.4 %copy-start = (bf16[16,64,128]{2,1,0:T(8,128)(2,1)}, bf16[16,64,128]{2,1,0:T(8,128)(2,1)S(1)}, u32[]{:S(2)}) copy-start(bf16[16,64,128]{2,1,0:T(8,128)(2,1)S(1)} %get-tuple-element.40.own_ref) | copy-start | bytes 786436
  3.9 111.6 %collective-permute-start.1 = (bf16[16,64,128]{2,1,0:T(8,128)(2,1)S(1)}, bf16[16,64,128]{2,1,0:T(8,128)(2,1)S(1)}, u32[]{:S(2)}, u32[]{:S(2)}) collective-permute-start(bf16[16,64,128]{2,1,0:T(8,128)(2,1)S(1)} %get-tuple-element.40.own_ref), channel_id=1, source_target_pairs={{0,28},{4,0},{8,4},{12,8},{16,12},{20,16},{24,20},{28,24},{1,29},{... | collective-permute-start | bytes 786440 | tf_op jit(solution)/shard_map/ppermute | solution.py:375
  4.4 111.1 %collective-permute-start = (bf16[16,64,128]{2,1,0:T(8,128)(2,1)S(1)}, bf16[16,64,128]{2,1,0:T(8,128)(2,1)S(1)}, u32[]{:S(2)}, u32[]{:S(2)}) collective-permute-start(bf16[16,64,128]{2,1,0:T(8,128)(2,1)S(1)} %get-tuple-element.40.own_ref), channel_id=1, source_target_pairs={{0,4},{4,8},{8,12},{12,16},{16,20},{20,24},{24,28},{28,0},{1,5},{5... | collective-permute-start | bytes 786440 | tf_op jit(solution)/shard_map/ppermute | solution.py:374
  115.5 0.7 copy-start.1
  115.5 0.8 copy-start.2
  136.6 10.4 %collective-permute-start.3 = (bf16[16,64,128]{2,1,0:T(8,128)(2,1)}, bf16[16,64,128]{2,1,0:T(8,128)(2,1)S(1)}, u32[]{:S(2)}, u32[]{:S(2)}) collective-permute-start(bf16[16,64,128]{2,1,0:T(8,128)(2,1)} %get-tuple-element.19.own_ref), channel_id=1, source_target_pairs={{0,28},{4,0},{8,4},{12,8},{16,12},{20,16},{24,20},{28,24},{1,29},{... | collective-permute-start | bytes 786440 | tf_op jit(solution)/shard_map/ppermute | solution.py:375
  136.6 14.5 %collective-permute-start.2 = (bf16[16,64,128]{2,1,0:T(8,128)(2,1)}, bf16[16,64,128]{2,1,0:T(8,128)(2,1)S(1)}, u32[]{:S(2)}, u32[]{:S(2)}) collective-permute-start(bf16[16,64,128]{2,1,0:T(8,128)(2,1)} %get-tuple-element.19.own_ref), channel_id=1, source_target_pairs={{0,4},{4,8},{8,12},{12,16},{16,20},{20,24},{24,28},{28,0},{1,5},{5... | collective-permute-start | bytes 786440 | tf_op jit(solution)/shard_map/ppermute | solution.py:374
  147.0 4.1 %copy-start.5 = (bf16[16,64,128]{2,1,0:T(8,128)(2,1)}, bf16[16,64,128]{2,1,0:T(8,128)(2,1)S(1)}, u32[]{:S(2)}) copy-start(bf16[16,64,128]{2,1,0:T(8,128)(2,1)S(1)} %collective-permute-done.3.high_ref) | copy-start | bytes 786436
  151.1 0.7 copy-start.6
  162.8 10.4 %collective-permute-start.5 = (bf16[16,64,128]{2,1,0:T(8,128)(2,1)}, bf16[16,64,128]{2,1,0:T(8,128)(2,1)S(1)}, u32[]{:S(2)}, u32[]{:S(2)}) collective-permute-start(bf16[16,64,128]{2,1,0:T(8,128)(2,1)} %get-tuple-element.24.own_ref), channel_id=1, source_target_pairs={{0,28},{4,0},{8,4},{12,8},{16,12},{20,16},{24,20},{28,24},{1,29},{... | collective-permute-start | bytes 786440 | tf_op jit(solution)/shard_map/ppermute | solution.py:375
  162.8 13.6 %collective-permute-start.4 = (bf16[16,64,128]{2,1,0:T(8,128)(2,1)}, bf16[16,64,128]{2,1,0:T(8,128)(2,1)S(1)}, u32[]{:S(2)}, u32[]{:S(2)}) collective-permute-start(bf16[16,64,128]{2,1,0:T(8,128)(2,1)} %get-tuple-element.24.own_ref), channel_id=1, source_target_pairs={{0,4},{4,8},{8,12},{12,16},{16,20},{20,24},{24,28},{28,0},{1,5},{5... | collective-permute-start | bytes 786440 | tf_op jit(solution)/shard_map/ppermute | solution.py:374
  173.2 3.3 %copy-start.3 = (bf16[16,64,128]{2,1,0:T(8,128)(2,1)}, bf16[16,64,128]{2,1,0:T(8,128)(2,1)S(1)}, u32[]{:S(2)}) copy-start(bf16[16,64,128]{2,1,0:T(8,128)(2,1)S(1)} %collective-permute-done.5.high_ref) | copy-start | bytes 786436
  176.5 0.7 copy-start.4
  188.2 9.8 %collective-permute-start.7 = (bf16[16,64,128]{2,1,0:T(8,128)(2,1)}, bf16[16,64,128]{2,1,0:T(8,128)(2,1)S(1)}, u32[]{:S(2)}, u32[]{:S(2)}) collective-permute-start(bf16[16,64,128]{2,1,0:T(8,128)(2,1)} %get-tuple-element.29.own_ref), channel_id=1, source_target_pairs={{0,28},{4,0},{8,4},{12,8},{16,12},{20,16},{24,20},{28,24},{1,29},{... | collective-permute-start | bytes 786440 | tf_op jit(solution)/shard_map/ppermute | solution.py:375
  188.3 13.2 %collective-permute-start.6 = (bf16[16,64,128]{2,1,0:T(8,128)(2,1)}, bf16[16,64,128]{2,1,0:T(8,128)(2,1)S(1)}, u32[]{:S(2)}, u32[]{:S(2)}) collective-permute-start(bf16[16,64,128]{2,1,0:T(8,128)(2,1)} %get-tuple-element.29.own_ref), channel_id=1, source_target_pairs={{0,4},{4,8},{8,12},{12,16},{16,20},{20,24},{24,28},{28,0},{1,5},{5... | collective-permute-start | bytes 786440 | tf_op jit(solution)/shard_map/ppermute | solution.py:374
  198.0 4.1 %copy-start.7 = (bf16[16,64,128]{2,1,0:T(8,128)(2,1)}, bf16[16,64,128]{2,1,0:T(8,128)(2,1)S(1)}, u32[]{:S(2)}) copy-start(bf16[16,64,128]{2,1,0:T(8,128)(2,1)S(1)} %collective-permute-done.7.high_ref) | copy-start | bytes 786436
  201.5 0.7 copy-start.8
where the time goes:
time: 213 us; the launch traced here: 212 us
  Pallas kernels  174 us (82%)
  starting transfers between devices  11.8 us (6%)
  waiting for transfers between devices  10.9 us (5%)
  other arithmetic  7.7 us (4%)
  local copies, waits for them, and re-layouts  4.8 us (2%)
  between operations  3.14 us (1%)
    pallas_call x1, Pallas kernels, route(): pl.pallas_call(functools.partial(route_kernel, peers, sides, pieces), out...  85.6 us
    pallas_call x4, Pallas kernels, local(): pl.pallas_call(functools.partial(far_kernel, first_sweep, last, room), ou...  52.4 us
    pallas_call x4, Pallas kernels, local(): pl.pallas_call(functools.partial(near_kernel, first_sweep, room), out_sha...  31.9 us
    ppermute x4, starting transfers between devices, local(): low_rows = lax.ppermute(rounded, 'rows', forward)  11.2 us
    ppermute x4, waiting for transfers between devices, local(): low_rows = lax.ppermute(rounded, 'rows', forward)  10.9 us
  transfers between devices with their start and end apart: 8, of which 3 were waited for; matrix products, arithmetic and copies ran while one was open for 4% of the time, Pallas kernels for 57%

commit v1 on v0

--- a/solution.py
+++ b/solution.py
@@ -10,7 +10,9 @@
 ITERS = 4
 GROUP = 16
 BUFFERS = 4
-VMEM_LIMIT = 54 * 1024 * 1024
+BATCH = 4
+VMEM_LIMIT = 40 * 1024 * 1024
+SPARE = 2
 MESH = pl.DeviceIdType.MESH
 
 
@@ -60,7 +62,9 @@
     )(left, right, diag.T, dest, col, shift, row, jnp.full((1,), local_rows, jnp.int32))
 
 
-def route_kernel(peers, sides, pieces, send_ref, got_ref, own_sem, send_sems, recv_sems):
+def route_kernel(
+    peers, sides, pieces, send_ref, field_ref, got_ref, low_ref, high_ref, own_sem, send_sems, recv_sems, halo_sends, halo_recvs
+):
     me, side = lax.axis_index("rows"), lax.axis_index("rhs")
     across, beside = side ^ 2, side ^ 1
     paired = peers & (peers - 1) == 0
@@ -113,6 +117,20 @@
         follow.update(zip(queue, queue[2:]))
     for item in far[:2] + near[:2]:
         to_owner(*item).start()
+
+    def halo(end, ref, step):
+        return pltpu.make_async_remote_copy(
+            src_ref=field_ref,
+            dst_ref=ref,
+            send_sem=halo_sends.at[end],
+            recv_sem=halo_recvs.at[end],
+            device_id=(lax.rem(me + step, peers), side),
+            device_id_type=MESH,
+        )
+
+    halos = [halo(0, low_ref, 1), halo(1, high_ref, peers - 1)]
+    for copy in halos:
+        copy.start()
     own = pltpu.make_async_copy(send_ref.at[me], got_ref.at[me * sides + side], own_sem)
     own.start()
     order = [(0, p) for p in range(count)]
@@ -133,6 +151,8 @@
             to_across(*order[step - 2]).wait_recv()
             on_beside(*order[step - 2]).start()
     own.wait()
+    for copy in halos:
+        copy.wait()
     for item in order:
         if item[0] > 0 and item not in follow:
             to_owner(*item).wait_send()
@@ -141,7 +161,7 @@
         on_beside(*item).wait()
 
 
-def route(send, peers, sides, room):
+def route(send, field, peers, sides, room):
     rows, width = send.shape[1:]
     if peers > 16 or room < 2:
         pieces = ((0, rows),)
@@ -149,17 +169,23 @@
         pieces = ((0, room // 2 * width), (room // 2 * width, rows))
     return pl.pallas_call(
         functools.partial(route_kernel, peers, sides, pieces),
-        out_shape=jax.ShapeDtypeStruct((peers * sides, rows, width), send.dtype),
-        in_specs=[pl.BlockSpec(memory_space=pltpu.HBM)],
-        out_specs=pl.BlockSpec(memory_space=pltpu.HBM),
+        out_shape=[
+            jax.ShapeDtypeStruct((SPARE * peers * sides, rows, width), send.dtype),
+            jax.ShapeDtypeStruct(field.shape, field.dtype),
+            jax.ShapeDtypeStruct(field.shape, field.dtype),
+        ],
+        in_specs=[pl.BlockSpec(memory_space=pltpu.HBM)] * 2,
+        out_specs=[pl.BlockSpec(memory_space=pltpu.HBM)] * 3,
         scratch_shapes=[
             pltpu.SemaphoreType.DMA,
             pltpu.SemaphoreType.DMA((4, peers, len(pieces))),
             pltpu.SemaphoreType.DMA((4, peers, len(pieces))),
+            pltpu.SemaphoreType.DMA((2,)),
+            pltpu.SemaphoreType.DMA((2,)),
         ],
         compiler_params=pltpu.CompilerParams(collective_id=0, has_side_effects=True),
         name="route",
-    )(send)
+    )(send, field)
 
 
 def block_lists(notes, room, local_rows):
@@ -199,14 +225,16 @@
     width = buf.shape[-1]
     chunks = lax.div(count_ref[0] + (GROUP - 1), jnp.int32(GROUP))
 
+    def whole(chunk):
+        slot = lax.rem(chunk, BUFFERS)
+        return pltpu.make_async_copy(
+            packed_ref.at[pl.ds(chunk * GROUP * width, GROUP * width)], buf.at[slot], sems.at[slot, 0]
+        )
+
     def copies(chunk):
+        if not first_sweep:
+            return [whole(chunk)]
         slot = lax.rem(chunk, BUFFERS)
-        if not first_sweep:
-            return [
-                pltpu.make_async_copy(
-                    packed_ref.at[pl.ds(chunk * GROUP * width, GROUP * width)], buf.at[slot], sems.at[slot, 0]
-                )
-            ]
         out = []
         for g in range(GROUP):
             item = list_ref[chunk * GROUP + g] >> (index_bits + col_bits)
@@ -216,7 +244,7 @@
                 pltpu.make_async_copy(
                     blocks_ref.at[part, pl.ds(pl.multiple_of(place * width, width), width)],
                     buf.at[slot, g * width : (g + 1) * width],
-                    sems.at[slot, g],
+                    sems.at[slot, 0],
                 )
             )
         return out
@@ -224,7 +252,7 @@
     def write(chunk):
         slot = lax.rem(chunk, BUFFERS)
         return pltpu.make_async_copy(
-            buf.at[slot], packed_ref.at[pl.ds(chunk * GROUP * width, GROUP * width)], sems.at[slot, GROUP]
+            buf.at[slot], packed_ref.at[pl.ds(chunk * GROUP * width, GROUP * width)], sems.at[slot, 1]
         )
 
     def start(chunk):
@@ -244,19 +272,22 @@
                 write(chunk - 1).wait()
 
         start(chunk + (BUFFERS - 1))
-        for copy in copies(chunk):
-            copy.wait()
+        whole(chunk).wait()
         if first_sweep:
             write(chunk).start()
         slot = lax.rem(chunk, BUFFERS)
         mask = (1 << index_bits) - 1
-        for g in range(0, GROUP, 2):
-            item = list_ref[chunk * GROUP + g]
-            other = list_ref[chunk * GROUP + g + 1]
-            col = (item >> index_bits) & ((1 << col_bits) - 1)
-            rows = jnp.concatenate([ext[item & mask], ext[other & mask]], axis=1)
-            pair = buf[slot, g * width : (g + 2) * width]
-            acc[col] += jnp.dot(rows, pair, preferred_element_type=jnp.float32)
+        for begin in range(0, GROUP, 2 * BATCH):
+            products = []
+            for g in range(begin, begin + 2 * BATCH, 2):
+                item = list_ref[chunk * GROUP + g]
+                other = list_ref[chunk * GROUP + g + 1]
+                rows = jnp.concatenate([ext[item & mask], ext[other & mask]], axis=1)
+                pair = buf[slot, g * width : (g + 2) * width]
+                col = (item >> index_bits) & ((1 << col_bits) - 1)
+                products.append((col, jnp.dot(rows, pair, preferred_element_type=jnp.float32)))
+            for col, product in products:
+                acc[col] += product
         return carry
 
     lax.fori_loop(0, chunks, body, 0)
@@ -281,27 +312,24 @@
     out_ref[...] = acc[0:rows]
 
 
-def far_kernel(first_sweep, last, room, list_ref, count_ref, coef_ref, blocks_ref, low_ref, high_ref, part_ref, *rest):
-    *refs, ext, acc, buf, sems, ext_sems = rest
+def far_kernel(sweep, room, list_ref, count_ref, coef_ref, blocks_ref, low_ref, high_ref, part_ref, *rest):
+    first_sweep, last = sweep == 0, sweep + 1 == ITERS
+    *refs, ext, acc, buf, sems = rest
     packed_ref = refs.pop() if first_sweep else blocks_ref
     if last:
         (res_out,) = refs
     else:
         dir_ref, adj_ref, res_out, dir_out, adj_out, round_out = refs
     rows = part_ref.shape[0]
-    low = pltpu.make_async_copy(low_ref, ext.at[0:rows], ext_sems.at[0])
-    high = pltpu.make_async_copy(high_ref, ext.at[rows : 2 * rows], ext_sems.at[1])
-    low.start()
-    high.start()
     acc[0:rows] = part_ref[...]
-    ext[2 * rows] = jnp.zeros_like(part_ref[0]).astype(jnp.bfloat16)
-    low.wait()
-    high.wait()
+    ext[0:rows] = low_ref[...]
+    ext[rows : 2 * rows] = high_ref[...]
+    ext[2 * rows] = jnp.zeros_like(ext[0])
     add_blocks(first_sweep, room, list_ref, count_ref, blocks_ref, packed_ref, ext, acc, buf, sems, rows)
     res = acc[0:rows]
     res_out[...] = res
     if not last:
-        direction = coef_ref[0] * dir_ref[...] + coef_ref[1] * res
+        direction = coef_ref[2 * sweep] * dir_ref[...] + coef_ref[2 * sweep + 1] * res
         dir_out[...] = direction
         adj_out[...] = adj_ref[...] + direction
         round_out[...] = direction.astype(jnp.bfloat16)
@@ -330,10 +358,11 @@
     send = form(
         factor_left, factor_right, state_diag, dest, col_local, row_shift, row_local, local_rows, peers, room
     )
-    got = route(send, peers, sides, room)
-    notes = got[:, room * width :, :].astype(jnp.int32)
+    rounded = (rhs_in / ((high_bound[0] + low_bound[0]) / 2.0)).astype(jnp.bfloat16)
+    got, low_rows, high_rows = route(send, rounded, peers, sides, room)
+    notes = got[: peers * sides, room * width :, :].astype(jnp.int32)
     near_list, near_count, far_list, far_count = block_lists(notes, room, local_rows)
-    packed_shape = jax.ShapeDtypeStruct((near_list.shape[0] * width, width), jnp.bfloat16)
+    packed_shape = jax.ShapeDtypeStruct((SPARE * near_list.shape[0] * width, width), jnp.bfloat16)
 
     low = low_bound[0]
     high = high_bound[0]
@@ -344,20 +373,24 @@
     residual = rhs_in
     direction = residual / theta
     adjoint = direction
-    rounded = direction.astype(jnp.bfloat16)
+    coefs = []
+    for _ in range(ITERS - 1):
+        rho_next = 1.0 / (2.0 * sigma - rho)
+        coefs += [rho_next * rho, 2.0 * rho_next / delta]
+        rho = rho_next
+    coefs = jnp.stack(coefs)
 
     forward = [(i, (i + 1) % peers) for i in range(peers)]
     backward = [(i, (i - 1) % peers) for i in range(peers)]
     smem = pl.BlockSpec(memory_space=pltpu.SMEM)
     vmem = pl.BlockSpec(memory_space=pltpu.VMEM)
     hbm = pl.BlockSpec(memory_space=pltpu.HBM)
-    anywhere = pl.BlockSpec(memory_space=pl.ANY)
     field = jax.ShapeDtypeStruct(rhs_in.shape, jnp.float32)
     work = [
         pltpu.VMEM((2 * local_rows + 1, columns, width), jnp.bfloat16),
         pltpu.VMEM((local_rows + 1, columns, width), jnp.float32),
         pltpu.VMEM((BUFFERS, GROUP * width, width), jnp.bfloat16),
-        pltpu.SemaphoreType.DMA((BUFFERS, GROUP + 1)),
+        pltpu.SemaphoreType.DMA((BUFFERS, 2)),
     ]
     params = pltpu.CompilerParams(vmem_limit_bytes=VMEM_LIMIT)
 
@@ -371,8 +404,9 @@
     near_blocks, far_blocks = got, got
     for sweep in range(ITERS):
         first_sweep, last = sweep == 0, sweep + 1 == ITERS
-        low_rows = lax.ppermute(rounded, "rows", forward)
-        high_rows = lax.ppermute(rounded, "rows", backward)
+        if not first_sweep:
+            low_rows = lax.ppermute(rounded, "rows", forward)
+            high_rows = lax.ppermute(rounded, "rows", backward)
         result = pl.pallas_call(
             functools.partial(near_kernel, first_sweep, room),
             out_shape=[field] + [packed_shape] * first_sweep,
@@ -386,24 +420,18 @@
         part = result[0]
         if first_sweep:
             near_blocks = result[1]
-        if last:
-            coef = jnp.zeros((2,), jnp.float32)
-        else:
-            rho_next = 1.0 / (2.0 * sigma - rho)
-            coef = jnp.stack([rho_next * rho, 2.0 * rho_next / delta])
-            rho = rho_next
         fields = [] if last else [direction, adjoint]
         outs = [field] if last else [field] * 3 + [jax.ShapeDtypeStruct(rhs_in.shape, jnp.bfloat16)]
         result = pl.pallas_call(
-            functools.partial(far_kernel, first_sweep, last, room),
+            functools.partial(far_kernel, sweep, room),
             out_shape=outs + [packed_shape] * first_sweep,
-            in_specs=[smem, smem, smem, hbm, anywhere, anywhere, vmem] + [vmem] * len(fields),
+            in_specs=[smem, smem, smem, hbm, vmem, vmem, vmem] + [vmem] * len(fields),
             out_specs=[vmem] * len(outs) + [hbm] * first_sweep,
-            scratch_shapes=work + [pltpu.SemaphoreType.DMA((2,))],
+            scratch_shapes=work,
             compiler_params=params,
             cost_estimate=cost(near_list.shape[0] // 2),
             name="far_last" if last else "far_first" if first_sweep else "far",
-        )(far_list, far_count, coef, far_blocks, low_rows, high_rows, part, *fields)
+        )(far_list, far_count, coefs, far_blocks, low_rows, high_rows, part, *fields)
         residual = result[0]
         if first_sweep:
             far_blocks = result[-1]

time: 213 us -> 200 us (0.939)
  the two profiles are of different devices: /device:TPU:12 before, /device:TPU:0 now
where the time goes in v1:
time: 200 us; the launch traced here: 197 us
  Pallas kernels  124 us (62%)
  starting transfers between devices  30.6 us (15%)
  waiting for transfers between devices  24 us (12%)
  local copies, waits for them, and re-layouts  10.1 us (5%)
  other arithmetic  5.26 us (3%)
  between operations  3.1 us (2%)
    pallas_call x1, Pallas kernels, route(): pl.pallas_call(functools.partial(route_kernel, peers, sides, pieces), out...  87.9 us
    ppermute x3, starting transfers between devices, local(): low_rows = lax.ppermute(rounded, 'rows', forward)  30.5 us
    pallas_call x4, Pallas kernels, local(): pl.pallas_call(functools.partial(far_kernel, sweep, room), out_shape=outs...  20.3 us
    ppermute x3, waiting for transfers between devices, local(): high_rows = lax.ppermute(rounded, 'rows', backward)  17.4 us
    pallas_call x4, Pallas kernels, local(): pl.pallas_call(functools.partial(near_kernel, first_sweep, room), out_sha...  14.1 us
    unnamed x23, local copies, waits for them, and re-layouts  9.54 us
    ppermute x3, waiting for transfers between devices, local(): low_rows = lax.ppermute(rounded, 'rows', forward)  6.57 us
  transfers between devices with their start and end apart: 6, of which 6 were waited for; matrix products, arithmetic and copies ran while one was open for 0% of the time, Pallas kernels for 5%

profile of v1, /device:TPU:0, one launch (start us, length us, event | category | flops | bytes accessed | tf_op | source)
XLA Modules:
  0.0 196.9 jit_solution(14711755990351033878)
XLA Ops:
  3.0 1.9 fusion.7
  4.8 1.2 copy-done.3
  6.0 1.2 copy-done.4
  9.9 1.5 form.1.send_ref
  11.4 1.7 copy-done
  13.0 87.9 %route.1 = (bf16[64,1552,128]{2,1,0:T(8,128)(2,1)}, bf16[16,64,128]{2,1,0:T(8,128)(2,1)}, bf16[16,64,128]{2,1,0:T(8,128)(2,1)}) custom-call(bf16[8,1552,128]{2,1,0:T(8,128)(2,1)} %copy-done, bf16[16,64,128]{2,1,0:T(8,128)(2,1)} %get-tuple-element.47.field_ref.own_ref), custom_call_target="tpu_custom_call" | custom-call | tf_op jit(solution)/shard_map/route/pallas_call | solution.py:170
  101.0 1.0 slice_convert_fusion
  105.7 0.9 copy-done.1
  106.6 1.0 copy-done.2
  107.6 5.1 %near_first.1 = (f32[16,64,128]{2,1,0:T(8,128)S(1)}, bf16[106496,128]{1,0:T(8,128)(2,1)}) custom-call(s32[416]{0:T(512)S(1)} %get-tuple-element.53.list_ref, s32[1]{0:T(128)} %bitcast.11.count_ref, bf16[64,1552,128]{2,1,0:T(8,128)(2,1)} %get-tuple-element.20.blocks_ref, bf16[16,64,128]{2,1,0:T(8,128)(2,1)S(1)} %copy-done.1, ...), custom_call_target="tpu_custom_call" | custom-call | flops 218103808 | bytes 5505024 | tf_op jit(solution)/shard_map/near_first/pallas_call | solution.py:410
  112.8 6.9 %far_first.1 = (f32[16,64,128]{2,1,0:T(8,128)S(1)}, f32[16,64,128]{2,1,0:T(8,128)S(1)}, f32[16,64,128]{2,1,0:T(8,128)S(1)}, bf16[16,64,128]{2,1,0:T(8,128)(2,1)S(1)}, bf16[106496,128]{1,0:T(8,128)(2,1)}) custom-call(s32[416]{0:T(512)S(1)} %get-tuple-element.54.list_ref, s32[1]{0:T(128)} %bitcast.3.count_ref, f32[6]{0:T(128)S(1)} %stack.27.coef_ref, ...), custom_call_target="tpu_custom_call" | custom-call | flops 436207616 | bytes 8912896 | tf_op jit(solution)/shard_map/far_first/pallas_call | solution.py:425
  119.8 18.3 %collective-permute-start = (bf16[16,64,128]{2,1,0:T(8,128)(2,1)S(1)}, bf16[16,64,128]{2,1,0:T(8,128)(2,1)S(1)}, u32[]{:S(2)}, u32[]{:S(2)}) collective-permute-start(bf16[16,64,128]{2,1,0:T(8,128)(2,1)S(1)} %get-tuple-element.25.own_ref), channel_id=1, source_target_pairs={{0,4},{4,8},{8,12},{12,16},{16,20},{20,24},{24,28},{28,0},{1,5},{5... | collective-permute-start | bytes 786440 | tf_op jit(solution)/shard_map/ppermute | solution.py:408
  138.1 3.0 %near.3.part_ref = f32[16,64,128]{2,1,0:T(8,128)S(1)} custom-call(s32[416]{0:T(512)S(1)} %get-tuple-element.53.list_ref, s32[1]{0:T(128)} %bitcast.11.count_ref, bf16[106496,128]{1,0:T(8,128)(2,1)} %get-tuple-element.26.blocks_ref, bf16[16,64,128]{2,1,0:T(8,128)(2,1)S(1)} %get-tuple-element.25.own_ref, f32[16,64,128]{2,1,0:T(8,128)S(1)} %get-tuple-element.27.dir_ref.rest_0_, ...), custom_call_target="tpu_custom_call" | custom-call | flops 218103808 | bytes 5505024 | tf_op jit(solution)/shard_map/near/pallas_call | solution.py:410
  141.1 3.7 %collective-permute-done.1.high_ref = bf16[16,64,128]{2,1,0:T(8,128)(2,1)S(1)} collective-permute-done((bf16[16,64,128]{2,1,0:T(8,128)(2,1)S(1)}, bf16[16,64,128]{2,1,0:T(8,128)(2,1)S(1)}, u32[]{:S(2)}, u32[]{:S(2)}) %collective-permute-start.1) | collective-permute-done | bytes 262176 | tf_op jit(solution)/shard_map/ppermute | solution.py:409
  144.9 4.9 %collective-permute-done.low_ref = bf16[16,64,128]{2,1,0:T(8,128)(2,1)S(1)} collective-permute-done((bf16[16,64,128]{2,1,0:T(8,128)(2,1)S(1)}, bf16[16,64,128]{2,1,0:T(8,128)(2,1)S(1)}, u32[]{:S(2)}, u32[]{:S(2)}) %collective-permute-start) | collective-permute-done | bytes 262176 | tf_op jit(solution)/shard_map/ppermute | solution.py:408
  149.8 4.0 %far.2 = (f32[16,64,128]{2,1,0:T(8,128)S(1)}, f32[16,64,128]{2,1,0:T(8,128)S(1)}, f32[16,64,128]{2,1,0:T(8,128)S(1)}, bf16[16,64,128]{2,1,0:T(8,128)(2,1)S(1)}) custom-call(s32[416]{0:T(512)S(1)} %get-tuple-element.54.list_ref, s32[1]{0:T(128)} %bitcast.3.count_ref, f32[6]{0:T(128)S(1)} %stack.27.coef_ref, bf16[106496,128]{1,0:T(8,128)(2,1)} %get-tuple-element.24.blocks_ref, ...), custom_call_target="tpu_custom_call" | custom-call | flops 436207616 | bytes 8912896 | tf_op jit(solution)/shard_map/far/pallas_call | solution.py:425
  153.9 6.1 %collective-permute-start.2 = (bf16[16,64,128]{2,1,0:T(8,128)(2,1)S(1)}, bf16[16,64,128]{2,1,0:T(8,128)(2,1)S(1)}, u32[]{:S(2)}, u32[]{:S(2)}) collective-permute-start(bf16[16,64,128]{2,1,0:T(8,128)(2,1)S(1)} %get-tuple-element.30.own_ref), channel_id=1, source_target_pairs={{0,4},{4,8},{8,12},{12,16},{16,20},{20,24},{24,28},{28,0},{1,5},{5... | collective-permute-start | bytes 786440 | tf_op jit(solution)/shard_map/ppermute | solution.py:408
  160.0 3.0 %near.4.part_ref = f32[16,64,128]{2,1,0:T(8,128)S(1)} custom-call(s32[416]{0:T(512)S(1)} %get-tuple-element.53.list_ref, s32[1]{0:T(128)} %bitcast.11.count_ref, bf16[106496,128]{1,0:T(8,128)(2,1)} %get-tuple-element.26.blocks_ref, bf16[16,64,128]{2,1,0:T(8,128)(2,1)S(1)} %get-tuple-element.30.own_ref, f32[16,64,128]{2,1,0:T(8,128)S(1)} %get-tuple-element.31.dir_ref.rest_0_, ...), custom_call_target="tpu_custom_call" | custom-call | flops 218103808 | bytes 5505024 | tf_op jit(solution)/shard_map/near/pallas_call | solution.py:410
  163.0 7.0 %collective-permute-done.3.high_ref = bf16[16,64,128]{2,1,0:T(8,128)(2,1)S(1)} collective-permute-done((bf16[16,64,128]{2,1,0:T(8,128)(2,1)S(1)}, bf16[16,64,128]{2,1,0:T(8,128)(2,1)S(1)}, u32[]{:S(2)}, u32[]{:S(2)}) %collective-permute-start.3) | collective-permute-done | bytes 262176 | tf_op jit(solution)/shard_map/ppermute | solution.py:409
  170.9 4.8 %far.3 = (f32[16,64,128]{2,1,0:T(8,128)S(1)}, f32[16,64,128]{2,1,0:T(8,128)S(1)}, f32[16,64,128]{2,1,0:T(8,128)}, bf16[16,64,128]{2,1,0:T(8,128)(2,1)S(1)}) custom-call(s32[416]{0:T(512)S(1)} %get-tuple-element.54.list_ref, s32[1]{0:T(128)} %bitcast.3.count_ref, f32[6]{0:T(128)S(1)} %stack.27.coef_ref, bf16[106496,128]{1,0:T(8,128)(2,1)} %get-tuple-element.24.blocks_ref, ...), custom_call_target="tpu_custom_call" | custom-call | flops 436207616 | bytes 8912896 | tf_op jit(solution)/shard_map/far/pallas_call | solution.py:425
  175.7 6.1 %collective-permute-start.4 = (bf16[16,64,128]{2,1,0:T(8,128)(2,1)S(1)}, bf16[16,64,128]{2,1,0:T(8,128)(2,1)S(1)}, u32[]{:S(2)}, u32[]{:S(2)}) collective-permute-start(bf16[16,64,128]{2,1,0:T(8,128)(2,1)S(1)} %get-tuple-element.35.own_ref), channel_id=1, source_target_pairs={{0,4},{4,8},{8,12},{12,16},{16,20},{20,24},{24,28},{28,0},{1,5},{5... | collective-permute-start | bytes 786440 | tf_op jit(solution)/shard_map/ppermute | solution.py:408
  181.8 3.0 %near.5.part_ref = f32[16,64,128]{2,1,0:T(8,128)S(1)} custom-call(s32[416]{0:T(512)S(1)} %get-tuple-element.53.list_ref, s32[1]{0:T(128)} %bitcast.11.count_ref, bf16[106496,128]{1,0:T(8,128)(2,1)} %get-tuple-element.26.blocks_ref, bf16[16,64,128]{2,1,0:T(8,128)(2,1)S(1)} %get-tuple-element.35.own_ref, f32[16,64,128]{2,1,0:T(8,128)S(1)} %get-tuple-element.36.dir_ref, ...), custom_call_target="tpu_custom_call" | custom-call | flops 218103808 | bytes 5505024 | tf_op jit(solution)/shard_map/near/pallas_call | solution.py:410
  184.8 6.7 %collective-permute-done.5.high_ref = bf16[16,64,128]{2,1,0:T(8,128)(2,1)S(1)} collective-permute-done((bf16[16,64,128]{2,1,0:T(8,128)(2,1)S(1)}, bf16[16,64,128]{2,1,0:T(8,128)(2,1)S(1)}, u32[]{:S(2)}, u32[]{:S(2)}) %collective-permute-start.5) | collective-permute-done | bytes 262176 | tf_op jit(solution)/shard_map/ppermute | solution.py:409
  192.2 4.7 %far_last.1 = f32[16,64,128]{2,1,0:T(8,128)} custom-call(s32[416]{0:T(512)S(1)} %get-tuple-element.54.list_ref, s32[1]{0:T(128)} %bitcast.3.count_ref, f32[6]{0:T(128)S(1)} %stack.27.coef_ref, bf16[106496,128]{1,0:T(8,128)(2,1)} %get-tuple-element.24.blocks_ref, bf16[16,64,128]{2,1,0:T(8,128)(2,1)S(1)} %collective-permute-done.4.low_ref, ...), custom_call_target="tpu_custom_call" | custom-call | flops 436207616 | bytes 8912896 | tf_op jit(solution)/shard_map/far_last/pallas_call | solution.py:425
  (40 shorter events, 8.2 us)
Async XLA Ops:
  4.8 1.2 copy-start.3
  6.0 1.2 copy-start.4
  7.3 0.7 copy-start.7
  7.9 0.7 copy-start.8
  8.6 0.7 copy-start.9
  9.2 0.7 copy-start.10
  11.4 1.7 copy-start
  101.0 11.9 %copy-start.5 = (bf16[16,64,128]{2,1,0:T(8,128)(2,1)S(1)}, bf16[16,64,128]{2,1,0:T(8,128)(2,1)}, u32[]{:S(2)}) copy-start(bf16[16,64,128]{2,1,0:T(8,128)(2,1)} %get-tuple-element.21.low_ref) | copy-start | bytes 786436
  101.0 11.9 %copy-start.6 = (bf16[16,64,128]{2,1,0:T(8,128)(2,1)S(1)}, bf16[16,64,128]{2,1,0:T(8,128)(2,1)}, u32[]{:S(2)}) copy-start(bf16[16,64,128]{2,1,0:T(8,128)(2,1)} %get-tuple-element.22.high_ref) | copy-start | bytes 786436
  105.6 1.0 copy-start.1
  106.6 1.0 copy-start.2
  119.7 25.2 %collective-permute-start.1 = (bf16[16,64,128]{2,1,0:T(8,128)(2,1)S(1)}, bf16[16,64,128]{2,1,0:T(8,128)(2,1)S(1)}, u32[]{:S(2)}, u32[]{:S(2)}) collective-permute-start(bf16[16,64,128]{2,1,0:T(8,128)(2,1)S(1)} %get-tuple-element.25.own_ref), channel_id=1, source_target_pairs={{0,28},{4,0},{8,4},{12,8},{16,12},{20,16},{24,20},{28,24},{1,29},{... | collective-permute-start | bytes 786440 | tf_op jit(solution)/shard_map/ppermute | solution.py:409
  119.8 30.0 %collective-permute-start = (bf16[16,64,128]{2,1,0:T(8,128)(2,1)S(1)}, bf16[16,64,128]{2,1,0:T(8,128)(2,1)S(1)}, u32[]{:S(2)}, u32[]{:S(2)}) collective-permute-start(bf16[16,64,128]{2,1,0:T(8,128)(2,1)S(1)} %get-tuple-element.25.own_ref), channel_id=1, source_target_pairs={{0,4},{4,8},{8,12},{12,16},{16,20},{20,24},{24,28},{28,0},{1,5},{5... | collective-permute-start | bytes 786440 | tf_op jit(solution)/shard_map/ppermute | solution.py:408
  153.8 16.2 %collective-permute-start.3 = (bf16[16,64,128]{2,1,0:T(8,128)(2,1)S(1)}, bf16[16,64,128]{2,1,0:T(8,128)(2,1)S(1)}, u32[]{:S(2)}, u32[]{:S(2)}) collective-permute-start(bf16[16,64,128]{2,1,0:T(8,128)(2,1)S(1)} %get-tuple-element.30.own_ref), channel_id=1, source_target_pairs={{0,28},{4,0},{8,4},{12,8},{16,12},{20,16},{24,20},{28,24},{1,29},{... | collective-permute-start | bytes 786440 | tf_op jit(solution)/shard_map/ppermute | solution.py:409
  153.9 17.0 %collective-permute-start.2 = (bf16[16,64,128]{2,1,0:T(8,128)(2,1)S(1)}, bf16[16,64,128]{2,1,0:T(8,128)(2,1)S(1)}, u32[]{:S(2)}, u32[]{:S(2)}) collective-permute-start(bf16[16,64,128]{2,1,0:T(8,128)(2,1)S(1)} %get-tuple-element.30.own_ref), channel_id=1, source_target_pairs={{0,4},{4,8},{8,12},{12,16},{16,20},{20,24},{24,28},{28,0},{1,5},{5... | collective-permute-start | bytes 786440 | tf_op jit(solution)/shard_map/ppermute | solution.py:408
  175.6 15.8 %collective-permute-start.5 = (bf16[16,64,128]{2,1,0:T(8,128)(2,1)S(1)}, bf16[16,64,128]{2,1,0:T(8,128)(2,1)S(1)}, u32[]{:S(2)}, u32[]{:S(2)}) collective-permute-start(bf16[16,64,128]{2,1,0:T(8,128)(2,1)S(1)} %get-tuple-element.35.own_ref), channel_id=1, source_target_pairs={{0,28},{4,0},{8,4},{12,8},{16,12},{20,16},{24,20},{28,24},{1,29},{... | collective-permute-start | bytes 786440 | tf_op jit(solution)/shard_map/ppermute | solution.py:409
  175.7 16.5 %collective-permute-start.4 = (bf16[16,64,128]{2,1,0:T(8,128)(2,1)S(1)}, bf16[16,64,128]{2,1,0:T(8,128)(2,1)S(1)}, u32[]{:S(2)}, u32[]{:S(2)}) collective-permute-start(bf16[16,64,128]{2,1,0:T(8,128)(2,1)S(1)} %get-tuple-element.35.own_ref), channel_id=1, source_target_pairs={{0,4},{4,8},{8,12},{12,16},{16,20},{20,24},{24,28},{28,0},{1,5},{5... | collective-permute-start | bytes 786440 | tf_op jit(solution)/shard_map/ppermute | solution.py:408

commit v2 on v1

--- a/solution.py
+++ b/solution.py
@@ -17,10 +17,10 @@
 
 
 def bits_of(local_rows):
-    return (2 * local_rows).bit_length(), local_rows.bit_length()
-
-
-def form_kernel(room, left_ref, right_ref, diag_ref, dest_ref, col_ref, shift_ref, row_ref, rows_ref, send_ref, notes, filled):
+    return (3 * local_rows).bit_length(), local_rows.bit_length()
+
+
+def form_kernel(room, left_ref, right_ref, diag_ref, place_ref, send_ref, notes, filled):
     slots, width, _ = left_ref.shape
     peers = send_ref.shape[0]
     notes[...] = jnp.zeros_like(notes)
@@ -31,27 +31,25 @@
     for k in range(slots):
         scaled = (diag_ref[:, k : k + 1] * right_ref[k].astype(jnp.float32)).astype(jnp.bfloat16)
         block = jnp.dot(left_ref[k], scaled, preferred_element_type=jnp.float32)
-        owner = dest_ref[k]
+        owner = place_ref[k]
         place = filled[owner]
         filled[owner] = place + 1
         send_ref[owner, pl.ds(pl.multiple_of(place * width, width), width)] = block.astype(jnp.bfloat16)
-        shift = shift_ref[k]
-        index = row_ref[k] + jnp.where(shift == 2, rows_ref[0], 0)
-        near = jnp.where(shift == 1, 1, 0)
-        note = jnp.where(line == 0, 1, jnp.where(line == 1, col_ref[k], jnp.where(line == 2, index, near)))
-        notes[owner] = jnp.where((lane == place) & (line < 4), note, notes[owner])
+        col, index = place_ref[slots + k], place_ref[2 * slots + k]
+        note = jnp.where(line == 0, 1, jnp.where(line == 1, col, index))
+        notes[owner] = jnp.where((lane == place) & (line < 3), note, notes[owner])
     for owner in range(peers):
         send_ref[owner, room * width : room * width + 16] = notes[owner].astype(jnp.float32).astype(jnp.bfloat16)
 
 
-def form(left, right, diag, dest, col, shift, row, local_rows, peers, room):
+def form(left, right, diag, places, peers, room):
     slots, width, _ = left.shape
     smem = pl.BlockSpec(memory_space=pltpu.SMEM)
     vmem = pl.BlockSpec(memory_space=pltpu.VMEM)
     return pl.pallas_call(
         functools.partial(form_kernel, room),
         out_shape=jax.ShapeDtypeStruct((peers, room * width + 16, width), jnp.bfloat16),
-        in_specs=[vmem, vmem, vmem, smem, smem, smem, smem, smem],
+        in_specs=[vmem, vmem, vmem, smem],
         out_specs=vmem,
         scratch_shapes=[
             pltpu.VMEM((peers, 16, width), jnp.int32),
@@ -59,7 +57,7 @@
         ],
         compiler_params=pltpu.CompilerParams(vmem_limit_bytes=VMEM_LIMIT),
         name="form",
-    )(left, right, diag.T, dest, col, shift, row, jnp.full((1,), local_rows, jnp.int32))
+    )(left, right, diag.T, places)
 
 
 def route_kernel(
@@ -174,8 +172,8 @@
             jax.ShapeDtypeStruct(field.shape, field.dtype),
             jax.ShapeDtypeStruct(field.shape, field.dtype),
         ],
-        in_specs=[pl.BlockSpec(memory_space=pltpu.HBM)] * 2,
-        out_specs=[pl.BlockSpec(memory_space=pltpu.HBM)] * 3,
+        in_specs=[pl.BlockSpec(memory_space=pl.ANY)] * 2,
+        out_specs=[pl.BlockSpec(memory_space=pltpu.HBM)] + [pl.BlockSpec(memory_space=pl.ANY)] * 2,
         scratch_shapes=[
             pltpu.SemaphoreType.DMA,
             pltpu.SemaphoreType.DMA((4, peers, len(pieces))),
@@ -188,42 +186,34 @@
     )(send, field)
 
 
-def block_lists(notes, room, local_rows):
+def block_list(notes, room, rows_each, local_rows):
     index_bits, col_bits = bits_of(local_rows)
-    filled, col, index, near = [notes[:, i, :room].reshape(-1) for i in range(4)]
+    filled, col, index = [notes[:, i, :room].reshape(-1) for i in range(3)]
     count = filled.shape[0]
-    length = -(-(count + 2 * local_rows) // GROUP) * GROUP
-    key = jnp.where(filled == 1, (1 - near) * local_rows + col, -1)
+    length = -(-(count + local_rows) // GROUP) * GROUP
+    key = jnp.where(filled == 1, col, -1)
     items = jnp.arange(count)
-    keys = jnp.arange(2 * local_rows)
+    starts = (items // room * rows_each + items % room * notes.shape[2]) // 16
+    keys = jnp.arange(local_rows)
     rank = jnp.sum(
         ((key[:, None] == key[None, :]) & (items[None, :] < items[:, None])).astype(jnp.int32), axis=1
     )
     is_key = key[:, None] == keys[None, :]
     even = (jnp.sum(is_key.astype(jnp.int32), axis=0) + 1) // 2 * 2
-    near_key = keys < local_rows
-    before = (keys[:, None] > keys[None, :]) & (near_key[:, None] == near_key[None, :])
-    first = jnp.sum(jnp.where(before, even[None, :], 0), axis=1)
+    first = jnp.sum(jnp.where(keys[:, None] > keys[None, :], even[None, :], 0), axis=1)
     pos = rank + jnp.sum(jnp.where(is_key, first[None, :], 0), axis=1)
-    value = ((items << col_bits) | col) << index_bits | index
-    some = jnp.max(jnp.where(filled == 1, items, 0))
-    empty = ((some << col_bits) | local_rows) << index_bits | (2 * local_rows)
-
-    def listed(chosen):
-        pick = jnp.arange(length)[:, None] == jnp.where(chosen, pos, -1)[None, :]
-        return empty + jnp.sum(jnp.where(pick, value[None, :] - empty, 0), axis=1)
-
-    near_half = listed((key >= 0) & (key < local_rows))
-    far_half = listed(key >= local_rows)
-    near_count = jnp.sum(jnp.where(near_key, even, 0)).reshape(1)
-    far_count = jnp.sum(jnp.where(near_key, 0, even)).reshape(1)
-    return near_half, near_count, far_half, far_count
-
-
-def add_blocks(first_sweep, room, list_ref, count_ref, blocks_ref, packed_ref, ext, acc, buf, sems, local_rows):
+    value = ((starts << col_bits) | col) << index_bits | index
+    some = jnp.max(jnp.where(filled == 1, starts, 0))
+    empty = ((some << col_bits) | local_rows) << index_bits | (3 * local_rows)
+    pick = jnp.arange(length)[:, None] == jnp.where(key >= 0, pos, -1)[None, :]
+    listed = empty + jnp.sum(jnp.where(pick, value[None, :] - empty, 0), axis=1)
+    return jnp.concatenate([listed, jnp.sum(even).reshape(1)])
+
+
+def add_blocks(first_sweep, list_ref, blocks_ref, packed_ref, ext, acc, buf, sems, local_rows):
     index_bits, col_bits = bits_of(local_rows)
     width = buf.shape[-1]
-    chunks = lax.div(count_ref[0] + (GROUP - 1), jnp.int32(GROUP))
+    chunks = lax.div(list_ref[list_ref.shape[0] - 1] + (GROUP - 1), jnp.int32(GROUP))
 
     def whole(chunk):
         slot = lax.rem(chunk, BUFFERS)
@@ -237,12 +227,10 @@
         slot = lax.rem(chunk, BUFFERS)
         out = []
         for g in range(GROUP):
-            item = list_ref[chunk * GROUP + g] >> (index_bits + col_bits)
-            part = lax.div(item, jnp.int32(room))
-            place = item - part * room
+            begin = (list_ref[chunk * GROUP + g] >> (index_bits + col_bits)) * 16
             out.append(
                 pltpu.make_async_copy(
-                    blocks_ref.at[part, pl.ds(pl.multiple_of(place * width, width), width)],
+                    blocks_ref.at[pl.ds(pl.multiple_of(begin, 16), width)],
                     buf.at[slot, g * width : (g + 1) * width],
                     sems.at[slot, 0],
                 )
@@ -298,34 +286,21 @@
             write(chunks - 1).wait()
 
 
-def near_kernel(first_sweep, room, list_ref, count_ref, blocks_ref, own_ref, dir_ref, res_ref, *rest):
-    if first_sweep:
-        out_ref, packed_ref, ext, acc, buf, sems = rest
-    else:
-        out_ref, ext, acc, buf, sems = rest
-        packed_ref = blocks_ref
-    rows = dir_ref.shape[0]
-    acc[0:rows] = res_ref[...] - dir_ref[...]
-    ext[0:rows] = own_ref[...]
-    ext[2 * rows] = jnp.zeros_like(ext[0])
-    add_blocks(first_sweep, room, list_ref, count_ref, blocks_ref, packed_ref, ext, acc, buf, sems, rows)
-    out_ref[...] = acc[0:rows]
-
-
-def far_kernel(sweep, room, list_ref, count_ref, coef_ref, blocks_ref, low_ref, high_ref, part_ref, *rest):
+def sweep_kernel(sweep, list_ref, coef_ref, blocks_ref, low_ref, own_ref, high_ref, res_ref, dir_ref, *rest):
     first_sweep, last = sweep == 0, sweep + 1 == ITERS
     *refs, ext, acc, buf, sems = rest
     packed_ref = refs.pop() if first_sweep else blocks_ref
     if last:
         (res_out,) = refs
     else:
-        dir_ref, adj_ref, res_out, dir_out, adj_out, round_out = refs
-    rows = part_ref.shape[0]
-    acc[0:rows] = part_ref[...]
+        adj_ref, res_out, dir_out, adj_out, round_out = refs
+    rows = res_ref.shape[0]
+    acc[0:rows] = res_ref[...] - dir_ref[...]
     ext[0:rows] = low_ref[...]
-    ext[rows : 2 * rows] = high_ref[...]
-    ext[2 * rows] = jnp.zeros_like(ext[0])
-    add_blocks(first_sweep, room, list_ref, count_ref, blocks_ref, packed_ref, ext, acc, buf, sems, rows)
+    ext[rows : 2 * rows] = own_ref[...]
+    ext[2 * rows : 3 * rows] = high_ref[...]
+    ext[3 * rows] = jnp.zeros_like(ext[0])
+    add_blocks(first_sweep, list_ref, blocks_ref, packed_ref, ext, acc, buf, sems, rows)
     res = acc[0:rows]
     res_out[...] = res
     if not last:
@@ -333,6 +308,44 @@
         dir_out[...] = direction
         adj_out[...] = adj_ref[...] + direction
         round_out[...] = direction.astype(jnp.bfloat16)
+
+
+def halo_kernel(peers, field_ref, low_ref, high_ref, send_sems, recv_sems):
+    me, side = lax.axis_index("rows"), lax.axis_index("rhs")
+    after, before = lax.rem(me + 1, peers), lax.rem(me + peers - 1, peers)
+    barrier = pltpu.get_barrier_semaphore()
+    for other in (after, before):
+        pl.semaphore_signal(barrier, inc=1, device_id=(other, side), device_id_type=MESH)
+    pl.semaphore_wait(barrier, 2)
+
+    def copy(end, ref, other):
+        return pltpu.make_async_remote_copy(
+            src_ref=field_ref,
+            dst_ref=ref,
+            send_sem=send_sems.at[end],
+            recv_sem=recv_sems.at[end],
+            device_id=(other, side),
+            device_id_type=MESH,
+        )
+
+    copies = [copy(0, low_ref, after), copy(1, high_ref, before)]
+    for each in copies:
+        each.start()
+    for each in copies:
+        each.wait()
+
+
+def halo(field, peers):
+    vmem = pl.BlockSpec(memory_space=pltpu.VMEM)
+    return pl.pallas_call(
+        functools.partial(halo_kernel, peers),
+        out_shape=[jax.ShapeDtypeStruct(field.shape, field.dtype)] * 2,
+        in_specs=[vmem],
+        out_specs=[vmem] * 2,
+        scratch_shapes=[pltpu.SemaphoreType.DMA((2,)), pltpu.SemaphoreType.DMA((2,))],
+        compiler_params=pltpu.CompilerParams(collective_id=1, has_side_effects=True),
+        name="halo",
+    )(field)
 
 
 def local(
@@ -353,16 +366,15 @@
     width = factor_left.shape[1]
     local_rows, columns, _ = rhs_in.shape
     room = min(slots, max(2, 3 * slots // peers))
-    dest = owner[:, 0]
-
-    send = form(
-        factor_left, factor_right, state_diag, dest, col_local, row_shift, row_local, local_rows, peers, room
-    )
+
+    places = jnp.concatenate([owner[:, 0], col_local, row_shift * local_rows + row_local])
+    send = form(factor_left, factor_right, state_diag, places, peers, room)
     rounded = (rhs_in / ((high_bound[0] + low_bound[0]) / 2.0)).astype(jnp.bfloat16)
     got, low_rows, high_rows = route(send, rounded, peers, sides, room)
     notes = got[: peers * sides, room * width :, :].astype(jnp.int32)
-    near_list, near_count, far_list, far_count = block_lists(notes, room, local_rows)
-    packed_shape = jax.ShapeDtypeStruct((SPARE * near_list.shape[0] * width, width), jnp.bfloat16)
+    where = block_list(notes, room, got.shape[1], local_rows)
+    packed_rows = (where.shape[0] - 1) * width
+    packed_shape = jax.ShapeDtypeStruct((SPARE * packed_rows, width), jnp.bfloat16)
 
     low = low_bound[0]
     high = high_bound[0]
@@ -380,61 +392,44 @@
         rho = rho_next
     coefs = jnp.stack(coefs)
 
-    forward = [(i, (i + 1) % peers) for i in range(peers)]
-    backward = [(i, (i - 1) % peers) for i in range(peers)]
     smem = pl.BlockSpec(memory_space=pltpu.SMEM)
     vmem = pl.BlockSpec(memory_space=pltpu.VMEM)
     hbm = pl.BlockSpec(memory_space=pltpu.HBM)
     field = jax.ShapeDtypeStruct(rhs_in.shape, jnp.float32)
     work = [
-        pltpu.VMEM((2 * local_rows + 1, columns, width), jnp.bfloat16),
+        pltpu.VMEM((3 * local_rows + 1, columns, width), jnp.bfloat16),
         pltpu.VMEM((local_rows + 1, columns, width), jnp.float32),
         pltpu.VMEM((BUFFERS, GROUP * width, width), jnp.bfloat16),
         pltpu.SemaphoreType.DMA((BUFFERS, 2)),
     ]
     params = pltpu.CompilerParams(vmem_limit_bytes=VMEM_LIMIT)
 
-    def cost(amount):
-        return pl.CostEstimate(
-            flops=2 * amount * columns * width * width,
-            bytes_accessed=amount * width * width * 2 + 4 * rhs_in.size * 4,
-            transcendentals=0,
-        )
-
-    near_blocks, far_blocks = got, got
+    cost = pl.CostEstimate(
+        flops=columns * width * packed_rows,
+        bytes_accessed=packed_rows * width + 4 * rhs_in.size * 4,
+        transcendentals=0,
+    )
+
+    blocks = got.reshape(-1, width)
     for sweep in range(ITERS):
         first_sweep, last = sweep == 0, sweep + 1 == ITERS
         if not first_sweep:
-            low_rows = lax.ppermute(rounded, "rows", forward)
-            high_rows = lax.ppermute(rounded, "rows", backward)
-        result = pl.pallas_call(
-            functools.partial(near_kernel, first_sweep, room),
-            out_shape=[field] + [packed_shape] * first_sweep,
-            in_specs=[smem, smem, hbm, vmem, vmem, vmem],
-            out_specs=[vmem] + [hbm] * first_sweep,
-            scratch_shapes=work,
-            compiler_params=params,
-            cost_estimate=cost(near_list.shape[0] // 4),
-            name="near_first" if first_sweep else "near",
-        )(near_list, near_count, near_blocks, rounded, direction, residual)
-        part = result[0]
-        if first_sweep:
-            near_blocks = result[1]
-        fields = [] if last else [direction, adjoint]
+            low_rows, high_rows = halo(rounded, peers)
+        fields = [residual, direction] if last else [residual, direction, adjoint]
         outs = [field] if last else [field] * 3 + [jax.ShapeDtypeStruct(rhs_in.shape, jnp.bfloat16)]
         result = pl.pallas_call(
-            functools.partial(far_kernel, sweep, room),
+            functools.partial(sweep_kernel, sweep),
             out_shape=outs + [packed_shape] * first_sweep,
-            in_specs=[smem, smem, smem, hbm, vmem, vmem, vmem] + [vmem] * len(fields),
+            in_specs=[smem, smem, hbm] + [vmem] * (3 + len(fields)),
             out_specs=[vmem] * len(outs) + [hbm] * first_sweep,
             scratch_shapes=work,
             compiler_params=params,
-            cost_estimate=cost(near_list.shape[0] // 2),
-            name="far_last" if last else "far_first" if first_sweep else "far",
-        )(far_list, far_count, coefs, far_blocks, low_rows, high_rows, part, *fields)
+            cost_estimate=cost,
+            name="sweep",
+        )(where, coefs, blocks, low_rows, rounded, high_rows, *fields)
         residual = result[0]
         if first_sweep:
-            far_blocks = result[-1]
+            blocks = result[-1]
         if not last:
             direction, adjoint, rounded = result[1:4]
     return (adjoint, residual)

time: 200 us -> 225 us (1.12)
  the two profiles are of different devices: /device:TPU:0 before, /device:TPU:8 now
where the time goes in v2:
time: 225 us; the launch traced here: 223 us
  Pallas kernels  193 us (86%)
  local copies, waits for them, and re-layouts  19.8 us (9%)
  other arithmetic  7.28 us (3%)
  between operations  3.06 us (1%)
    pallas_call x1, Pallas kernels, route(): pl.pallas_call(functools.partial(route_kernel, peers, sides, pieces), out...  92.3 us
    pallas_call x4, Pallas kernels, local(): pl.pallas_call(functools.partial(sweep_kernel, sweep), out_shape=outs + [...  53.4 us
    pallas_call x3, Pallas kernels, halo(): pl.pallas_call(functools.partial(halo_kernel, peers), out_shape=[jax.Shap...  45.8 us
    unnamed x39, local copies, waits for them, and re-layouts  19.4 us

profile of v2, /device:TPU:8, one launch (start us, length us, event | category | flops | bytes accessed | tf_op | source)
XLA Modules:
  0.0 223.1 jit_solution(4707586380855924993)
XLA Ops:
  4.6 1.9 fusion.24
  6.4 1.2 copy-done.9
  7.7 1.2 copy-done.10
  8.9 1.4 form.1.send_ref
  10.3 1.7 copy-done
  12.0 92.3 %route.1 = (bf16[64,1552,128]{2,1,0:T(8,128)(2,1)}, bf16[16,64,128]{2,1,0:T(8,128)(2,1)}, bf16[16,64,128]{2,1,0:T(8,128)(2,1)}) custom-call(bf16[8,1552,128]{2,1,0:T(8,128)(2,1)} %copy-done, bf16[16,64,128]{2,1,0:T(8,128)(2,1)} %get-tuple-element.51.field_ref.own_ref), custom_call_target="tpu_custom_call" | custom-call | tf_op jit(solution)/shard_map/route/pallas_call | solution.py:168
  104.3 0.9 slice_convert_fusion
  109.3 0.9 copy-done.1
  110.2 1.0 copy-done.2
  111.3 0.9 copy-done.11
  112.2 0.9 copy-done.12
  113.2 22.9 %sweep.4 = (f32[16,64,128]{2,1,0:T(8,128)S(1)}, f32[16,64,128]{2,1,0:T(8,128)S(1)}, f32[16,64,128]{2,1,0:T(8,128)S(1)}, bf16[16,64,128]{2,1,0:T(8,128)(2,1)S(1)}, bf16[102400,128]{1,0:T(8,128)(2,1)}) custom-call(s32[401]{0:T(512)S(1)} %pad_add_fusion.list_ref, f32[6]{0:T(128)S(1)} %stack.27.coef_ref, bf16[99328,128]{1,0:T(8,128)(2,1)} %bitcast.13, ...), custom_call_target="tpu_custom_call" | custom-call | flops 419430400 | bytes 8650752 | tf_op jit(solution)/shard_map/sweep/pallas_call | solution.py:420
  136.7 16.0 %halo.3 = (bf16[16,64,128]{2,1,0:T(8,128)(2,1)}, bf16[16,64,128]{2,1,0:T(8,128)(2,1)}) custom-call(bf16[16,64,128]{2,1,0:T(8,128)(2,1)} %copy-done.3), custom_call_target="tpu_custom_call" | custom-call | tf_op jit(solution)/shard_map/halo/pallas_call | solution.py:340
  153.7 0.9 copy-done.13
  154.6 0.9 copy-done.14
  155.6 9.7 %sweep.5 = (f32[16,64,128]{2,1,0:T(8,128)S(1)}, f32[16,64,128]{2,1,0:T(8,128)S(1)}, f32[16,64,128]{2,1,0:T(8,128)S(1)}, bf16[16,64,128]{2,1,0:T(8,128)(2,1)S(1)}) custom-call(s32[401]{0:T(512)S(1)} %pad_add_fusion.list_ref, f32[6]{0:T(128)S(1)} %stack.27.coef_ref, bf16[102400,128]{1,0:T(8,128)(2,1)} %get-tuple-element.27.blocks_ref, ...), custom_call_target="tpu_custom_call" | custom-call | flops 419430400 | bytes 8650752 | tf_op jit(solution)/shard_map/sweep/pallas_call | solution.py:420
  166.0 15.2 %halo.4 = (bf16[16,64,128]{2,1,0:T(8,128)(2,1)}, bf16[16,64,128]{2,1,0:T(8,128)(2,1)}) custom-call(bf16[16,64,128]{2,1,0:T(8,128)(2,1)} %copy-done.5), custom_call_target="tpu_custom_call" | custom-call | tf_op jit(solution)/shard_map/halo/pallas_call | solution.py:340
  182.1 0.9 copy-done.15
  183.1 0.9 copy-done.16
  184.0 10.5 %sweep.6 = (f32[16,64,128]{2,1,0:T(8,128)S(1)}, f32[16,64,128]{2,1,0:T(8,128)S(1)}, f32[16,64,128]{2,1,0:T(8,128)}, bf16[16,64,128]{2,1,0:T(8,128)(2,1)S(1)}) custom-call(s32[401]{0:T(512)S(1)} %pad_add_fusion.list_ref, f32[6]{0:T(128)S(1)} %stack.27.coef_ref, bf16[102400,128]{1,0:T(8,128)(2,1)} %get-tuple-element.27.blocks_ref, ...), custom_call_target="tpu_custom_call" | custom-call | flops 419430400 | bytes 8650752 | tf_op jit(solution)/shard_map/sweep/pallas_call | solution.py:420
  195.2 14.7 %halo.5 = (bf16[16,64,128]{2,1,0:T(8,128)(2,1)}, bf16[16,64,128]{2,1,0:T(8,128)(2,1)}) custom-call(bf16[16,64,128]{2,1,0:T(8,128)(2,1)} %copy-done.7), custom_call_target="tpu_custom_call" | custom-call | tf_op jit(solution)/shard_map/halo/pallas_call | solution.py:340
  210.8 0.9 copy-done.17
  211.8 0.9 copy-done.18
  212.7 10.4 %sweep.7 = f32[16,64,128]{2,1,0:T(8,128)} custom-call(s32[401]{0:T(512)S(1)} %pad_add_fusion.list_ref, f32[6]{0:T(128)S(1)} %stack.27.coef_ref, bf16[102400,128]{1,0:T(8,128)(2,1)} %get-tuple-element.27.blocks_ref, bf16[16,64,128]{2,1,0:T(8,128)(2,1)S(1)} %copy-done.17, bf16[16,64,128]{2,1,0:T(8,128)(2,1)S(1)} %copy-done.8, ...), custom_call_target="tpu_custom_call" | custom-call | flops 419430400 | bytes 8650752 | tf_op jit(solution)/shard_map/sweep/pallas_call | solution.py:420
  (44 shorter events, 10.7 us)
Async XLA Ops:
  6.4 1.2 copy-start.9
  7.7 1.2 copy-start.10
  10.3 1.7 copy-start
  109.3 1.0 copy-start.1
  110.2 1.0 copy-start.2
  111.3 0.9 copy-start.11
  112.2 0.9 copy-start.12
  136.0 0.7 copy-start.3
  152.7 1.0 copy-start.4
  153.7 0.9 copy-start.13
  154.6 0.9 copy-start.14
  165.3 0.7 copy-start.5
  181.2 1.0 copy-start.6
  182.1 0.9 copy-start.15
  183.1 0.9 copy-start.16
  194.5 0.7 copy-start.7
  209.9 1.0 copy-start.8
  210.8 0.9 copy-start.17
  211.8 0.9 copy-start.18

commit v3 on v2

--- a/solution.py
+++ b/solution.py
@@ -12,6 +12,7 @@
 BUFFERS = 4
 BATCH = 4
 VMEM_LIMIT = 40 * 1024 * 1024
+VMEM_SMALL = 16 * 1024 * 1024
 SPARE = 2
 MESH = pl.DeviceIdType.MESH
 
@@ -61,7 +62,7 @@
 
 
 def route_kernel(
-    peers, sides, pieces, send_ref, field_ref, got_ref, low_ref, high_ref, own_sem, send_sems, recv_sems, halo_sends, halo_recvs
+    peers, sides, pieces, send_ref, field_ref, got_ref, near_ref, beyond_ref, own_sem, send_sems, recv_sems, halo_sends, halo_recvs
 ):
     me, side = lax.axis_index("rows"), lax.axis_index("rhs")
     across, beside = side ^ 2, side ^ 1
@@ -116,17 +117,21 @@
     for item in far[:2] + near[:2]:
         to_owner(*item).start()
 
-    def halo(end, ref, step):
+    def halo(end, ref, other):
         return pltpu.make_async_remote_copy(
             src_ref=field_ref,
             dst_ref=ref,
             send_sem=halo_sends.at[end],
             recv_sem=halo_recvs.at[end],
-            device_id=(lax.rem(me + step, peers), side),
+            device_id=(other, side),
             device_id_type=MESH,
         )
 
-    halos = [halo(0, low_ref, 1), halo(1, high_ref, peers - 1)]
+    odd = lax.rem(me, 2)
+    halos = [
+        halo(0, near_ref, me + 1 - 2 * odd),
+        halo(1, beyond_ref, lax.rem(me - 1 + 2 * odd + peers, peers)),
+    ]
     for copy in halos:
         copy.start()
     own = pltpu.make_async_copy(send_ref.at[me], got_ref.at[me * sides + side], own_sem)
@@ -181,7 +186,9 @@
             pltpu.SemaphoreType.DMA((2,)),
             pltpu.SemaphoreType.DMA((2,)),
         ],
-        compiler_params=pltpu.CompilerParams(collective_id=0, has_side_effects=True),
+        compiler_params=pltpu.CompilerParams(
+            collective_id=0, has_side_effects=True, vmem_limit_bytes=VMEM_LIMIT
+        ),
         name="route",
     )(send, field)
 
@@ -189,6 +196,8 @@
 def block_list(notes, room, rows_each, local_rows):
     index_bits, col_bits = bits_of(local_rows)
     filled, col, index = [notes[:, i, :room].reshape(-1) for i in range(3)]
+    swap = lax.rem(lax.axis_index("rows"), 2) == 0
+    index = jnp.where(swap, (2 - index // local_rows) * local_rows + index % local_rows, index)
     count = filled.shape[0]
     length = -(-(count + local_rows) // GROUP) * GROUP
     key = jnp.where(filled == 1, col, -1)
@@ -286,7 +295,7 @@
             write(chunks - 1).wait()
 
 
-def sweep_kernel(sweep, list_ref, coef_ref, blocks_ref, low_ref, own_ref, high_ref, res_ref, dir_ref, *rest):
+def sweep_kernel(sweep, list_ref, coef_ref, blocks_ref, near_ref, own_ref, beyond_ref, res_ref, dir_ref, *rest):
     first_sweep, last = sweep == 0, sweep + 1 == ITERS
     *refs, ext, acc, buf, sems = rest
     packed_ref = refs.pop() if first_sweep else blocks_ref
@@ -296,9 +305,9 @@
         adj_ref, res_out, dir_out, adj_out, round_out = refs
     rows = res_ref.shape[0]
     acc[0:rows] = res_ref[...] - dir_ref[...]
-    ext[0:rows] = low_ref[...]
+    ext[0:rows] = near_ref[...]
     ext[rows : 2 * rows] = own_ref[...]
-    ext[2 * rows : 3 * rows] = high_ref[...]
+    ext[2 * rows : 3 * rows] = beyond_ref[...]
     ext[3 * rows] = jnp.zeros_like(ext[0])
     add_blocks(first_sweep, list_ref, blocks_ref, packed_ref, ext, acc, buf, sems, rows)
     res = acc[0:rows]
@@ -310,40 +319,52 @@
         round_out[...] = direction.astype(jnp.bfloat16)
 
 
-def halo_kernel(peers, field_ref, low_ref, high_ref, send_sems, recv_sems):
+def halo_kernel(peers, pieces, field_ref, near_ref, beyond_ref, send_sems, recv_sems):
     me, side = lax.axis_index("rows"), lax.axis_index("rhs")
-    after, before = lax.rem(me + 1, peers), lax.rem(me + peers - 1, peers)
+    odd = lax.rem(me, 2)
+    partner = me + 1 - 2 * odd
+    onward = lax.rem(me + 2 - 4 * odd + peers, peers)
+    back = lax.rem(me - 2 + 4 * odd + peers, peers)
     barrier = pltpu.get_barrier_semaphore()
-    for other in (after, before):
+    for other in (partner, back):
         pl.semaphore_signal(barrier, inc=1, device_id=(other, side), device_id_type=MESH)
     pl.semaphore_wait(barrier, 2)
-
-    def copy(end, ref, other):
+    depth = field_ref.shape[0] // pieces
+
+    def copy(kind, p, src, dst, other):
         return pltpu.make_async_remote_copy(
-            src_ref=field_ref,
-            dst_ref=ref,
-            send_sem=send_sems.at[end],
-            recv_sem=recv_sems.at[end],
+            src_ref=src.at[p * depth : (p + 1) * depth],
+            dst_ref=dst.at[p * depth : (p + 1) * depth],
+            send_sem=send_sems.at[kind, p],
+            recv_sem=recv_sems.at[kind, p],
             device_id=(other, side),
             device_id_type=MESH,
         )
 
-    copies = [copy(0, low_ref, after), copy(1, high_ref, before)]
-    for each in copies:
+    first = [copy(0, p, field_ref, near_ref, partner) for p in range(pieces)]
+    second = [copy(1, p, near_ref, beyond_ref, onward) for p in range(pieces)]
+    for each in first:
         each.start()
-    for each in copies:
-        each.wait()
+    for p in range(pieces):
+        first[p].wait_recv()
+        second[p].start()
+    for p in range(pieces):
+        first[p].wait_send()
+        second[p].wait()
 
 
 def halo(field, peers):
     vmem = pl.BlockSpec(memory_space=pltpu.VMEM)
+    pieces = 4 if field.shape[0] % 4 == 0 else 1
     return pl.pallas_call(
-        functools.partial(halo_kernel, peers),
+        functools.partial(halo_kernel, peers, pieces),
         out_shape=[jax.ShapeDtypeStruct(field.shape, field.dtype)] * 2,
         in_specs=[vmem],
         out_specs=[vmem] * 2,
-        scratch_shapes=[pltpu.SemaphoreType.DMA((2,)), pltpu.SemaphoreType.DMA((2,))],
-        compiler_params=pltpu.CompilerParams(collective_id=1, has_side_effects=True),
+        scratch_shapes=[pltpu.SemaphoreType.DMA((2, pieces)), pltpu.SemaphoreType.DMA((2, pieces))],
+        compiler_params=pltpu.CompilerParams(
+            collective_id=1, has_side_effects=True, vmem_limit_bytes=VMEM_SMALL
+        ),
         name="halo",
     )(field)
 
@@ -370,7 +391,7 @@
     places = jnp.concatenate([owner[:, 0], col_local, row_shift * local_rows + row_local])
     send = form(factor_left, factor_right, state_diag, places, peers, room)
     rounded = (rhs_in / ((high_bound[0] + low_bound[0]) / 2.0)).astype(jnp.bfloat16)
-    got, low_rows, high_rows = route(send, rounded, peers, sides, room)
+    got, near_rows, beyond_rows = route(send, rounded, peers, sides, room)
     notes = got[: peers * sides, room * width :, :].astype(jnp.int32)
     where = block_list(notes, room, got.shape[1], local_rows)
     packed_rows = (where.shape[0] - 1) * width
@@ -414,7 +435,7 @@
     for sweep in range(ITERS):
         first_sweep, last = sweep == 0, sweep + 1 == ITERS
         if not first_sweep:
-            low_rows, high_rows = halo(rounded, peers)
+            near_rows, beyond_rows = halo(rounded, peers)
         fields = [residual, direction] if last else [residual, direction, adjoint]
         outs = [field] if last else [field] * 3 + [jax.ShapeDtypeStruct(rhs_in.shape, jnp.bfloat16)]
         result = pl.pallas_call(
@@ -426,7 +447,7 @@
             compiler_params=params,
             cost_estimate=cost,
             name="sweep",
-        )(where, coefs, blocks, low_rows, rounded, high_rows, *fields)
+        )(where, coefs, blocks, near_rows, rounded, beyond_rows, *fields)
         residual = result[0]
         if first_sweep:
             blocks = result[-1]

time: 225 us -> 190 us (0.84)
  the two profiles are of different devices: /device:TPU:8 before, /device:TPU:0 now
where the time goes in v3:
time: 190 us; the launch traced here: 189 us
  Pallas kernels  174 us (92%)
  other arithmetic  6.56 us (3%)
  local copies, waits for them, and re-layouts  4.71 us (2%)
  between operations  3.01 us (2%)
    pallas_call x1, Pallas kernels, route(): pl.pallas_call(functools.partial(route_kernel, peers, sides, pieces), out...  87.5 us
    pallas_call x3, Pallas kernels, halo(): pl.pallas_call(functools.partial(halo_kernel, peers, pieces), out_shape=[...  67.7 us
    pallas_call x4, Pallas kernels, local(): pl.pallas_call(functools.partial(sweep_kernel, sweep), out_shape=outs + [...  17.9 us
    unnamed x7, local copies, waits for them, and re-layouts  4.3 us

profile of v3, /device:TPU:0, one launch (start us, length us, event | category | flops | bytes accessed | tf_op | source)
XLA Modules:
  0.0 188.8 jit_solution(1873169390751620415)
XLA Ops:
  2.3 0.7 multiply_add_fusion
  3.0 0.7 pad_add_fusion.1.place_ref
  3.8 0.8 copy.14
  4.6 1.1 fusion.30
  5.7 1.2 copy-done.1
  7.0 1.2 copy-done.2
  8.2 1.4 form.1.send_ref
  9.6 87.5 %route.1 = (bf16[64,1552,128]{2,1,0:T(8,128)(2,1)}, bf16[16,64,128]{2,1,0:T(8,128)(2,1)S(1)}, bf16[16,64,128]{2,1,0:T(8,128)(2,1)S(1)}) custom-call(bf16[8,1552,128]{2,1,0:T(8,128)(2,1)S(1)} %form.1.send_ref, bf16[16,64,128]{2,1,0:T(8,128)(2,1)S(1)} %get-tuple-element.51.field_ref.own_ref), custom_call_target="tpu_custom_call" | custom-call | tf_op jit(solution)/shard_map/route/pallas_call | solution.py:173
  97.1 0.9 slice_convert_fusion
  98.1 0.9 fusion.3
  100.0 0.1 convert_reduce_fusion.1
  100.1 0.6 fusion.28
  100.8 0.1 select_reduce_fusion.2
  101.0 0.2 convert_reduce_fusion
  101.2 0.2 select_reduce_fusion
  101.4 0.7 pad_add_fusion.list_ref
  102.1 1.0 copy-done
  103.2 6.3 %sweep.4 = (f32[16,64,128]{2,1,0:T(8,128)S(1)}, f32[16,64,128]{2,1,0:T(8,128)S(1)}, f32[16,64,128]{2,1,0:T(8,128)S(1)}, bf16[16,64,128]{2,1,0:T(8,128)(2,1)S(1)}, bf16[102400,128]{1,0:T(8,128)(2,1)}) custom-call(s32[401]{0:T(512)S(1)} %pad_add_fusion.list_ref, f32[6]{0:T(128)S(1)} %stack.27.coef_ref, bf16[99328,128]{1,0:T(8,128)(2,1)} %bitcast.13, ...), custom_call_target="tpu_custom_call" | custom-call | flops 419430400 | bytes 8650752 | tf_op jit(solution)/shard_map/sweep/pallas_call | solution.py:441
  109.4 37.2 %halo.3 = (bf16[16,64,128]{2,1,0:T(8,128)(2,1)S(1)}, bf16[16,64,128]{2,1,0:T(8,128)(2,1)S(1)}) custom-call(bf16[16,64,128]{2,1,0:T(8,128)(2,1)S(1)} %get-tuple-element.28.field_ref.own_ref), custom_call_target="tpu_custom_call" | custom-call | tf_op jit(solution)/shard_map/halo/pallas_call | solution.py:359
  146.7 3.4 %sweep.5 = (f32[16,64,128]{2,1,0:T(8,128)S(1)}, f32[16,64,128]{2,1,0:T(8,128)S(1)}, f32[16,64,128]{2,1,0:T(8,128)S(1)}, bf16[16,64,128]{2,1,0:T(8,128)(2,1)S(1)}) custom-call(s32[401]{0:T(512)S(1)} %pad_add_fusion.list_ref, f32[6]{0:T(128)S(1)} %stack.27.coef_ref, bf16[102400,128]{1,0:T(8,128)(2,1)} %get-tuple-element.27.blocks_ref, ...), custom_call_target="tpu_custom_call" | custom-call | flops 419430400 | bytes 8650752 | tf_op jit(solution)/shard_map/sweep/pallas_call | solution.py:441
  150.1 15.9 %halo.4 = (bf16[16,64,128]{2,1,0:T(8,128)(2,1)S(1)}, bf16[16,64,128]{2,1,0:T(8,128)(2,1)S(1)}) custom-call(bf16[16,64,128]{2,1,0:T(8,128)(2,1)S(1)} %get-tuple-element.34.field_ref.own_ref), custom_call_target="tpu_custom_call" | custom-call | tf_op jit(solution)/shard_map/halo/pallas_call | solution.py:359
  165.9 4.2 %sweep.6 = (f32[16,64,128]{2,1,0:T(8,128)S(1)}, f32[16,64,128]{2,1,0:T(8,128)S(1)}, f32[16,64,128]{2,1,0:T(8,128)}, bf16[16,64,128]{2,1,0:T(8,128)(2,1)S(1)}) custom-call(s32[401]{0:T(512)S(1)} %pad_add_fusion.list_ref, f32[6]{0:T(128)S(1)} %stack.27.coef_ref, bf16[102400,128]{1,0:T(8,128)(2,1)} %get-tuple-element.27.blocks_ref, ...), custom_call_target="tpu_custom_call" | custom-call | flops 419430400 | bytes 8650752 | tf_op jit(solution)/shard_map/sweep/pallas_call | solution.py:441
  170.1 14.6 %halo.5 = (bf16[16,64,128]{2,1,0:T(8,128)(2,1)S(1)}, bf16[16,64,128]{2,1,0:T(8,128)(2,1)S(1)}) custom-call(bf16[16,64,128]{2,1,0:T(8,128)(2,1)S(1)} %get-tuple-element.41.field_ref.own_ref), custom_call_target="tpu_custom_call" | custom-call | tf_op jit(solution)/shard_map/halo/pallas_call | solution.py:359
  184.7 4.1 %sweep.7 = f32[16,64,128]{2,1,0:T(8,128)} custom-call(s32[401]{0:T(512)S(1)} %pad_add_fusion.list_ref, f32[6]{0:T(128)S(1)} %stack.27.coef_ref, bf16[102400,128]{1,0:T(8,128)(2,1)} %get-tuple-element.27.blocks_ref, bf16[16,64,128]{2,1,0:T(8,128)(2,1)S(1)} %get-tuple-element.42.near_ref, bf16[16,64,128]{2,1,0:T(8,128)(2,1)S(1)} %get-tuple-element.41.field_ref.own_ref, ...), custom_call_target="tpu_custom_call" | custom-call | flops 419430400 | bytes 8650752 | tf_op jit(solution)/shard_map/sweep/pallas_call | solution.py:441
  (12 shorter events, 0.6 us)
Async XLA Ops:
  5.7 1.2 copy-start.1
  7.0 1.2 copy-start.2
  102.1 1.0 copy-start
